TPU v7x, 512 devices: a whole 4x4x16 slice. The times are simulated.
512 devices in a mesh: seq: 64 (over z, x), head: 2 (over core), dp: 4 (over y).
Axes of the slice: x: 4, y: 4, z: 16, core: 2. Of those that a mesh axis runs over, the one named last changes fastest.
Arguments:
- hidden: bfloat16 [4, 12288, 1024], P('dp', 'seq'), may hold values from -6 to 6
- norm_gain: float32 [1024], replicated, may hold values from 0.5 to 1.5
- projection: bfloat16 [3, 1024, 1024], P(None, None, 'head'), may hold values from -1 to 1
- upstream: bfloat16 [4, 12288, 1024], P('dp', 'seq', 'head'), may hold values from -6 to 6
- cluster: int32 [4, 12288, 1], P('dp', 'seq'), may hold values from 0 to 63; in each aligned block of 192 rows (0 to 191, 192 to 383, ..., all dimensions but the last counted through in order) at most 9 rows name the same one
Outputs:
- input_gradient: bfloat16 [4, 12288, 1024], P('dp', 'seq', 'head')
- gain_gradient: float32 [1024], P('head')
Inputs may be any that keep to these rules, and one draw needn't show every extreme that they name: Among the 192 tokens of one device no cluster is named more than 9 times, a bound that some block reaches.
All inputs are finite; a program needn't handle non-finite values.
Results may differ from a plain program's by a relative error of at most 0.01.
The roundings to bfloat16 on the way count: a program that leaves them out, or rounds other values in their place, can miss the bound.
Values may be sent and summed in bfloat16 or wider, within the bound.
No kernel may reach another device: no remote copies, remote signals or barrier semaphores. Data moves between devices by JAX's collectives and lax.ppermute only.
A program may use at most 64 MiB of HBM per device.

v0:
```python
import jax
import jax.numpy as jnp
from jax import lax
from jax.sharding import PartitionSpec as P

HDIM = 64
CLUS_DEV = 1


epsilon = 1e-05
masked = -1e30


def normalize(values, norm_gain):
    values = values.astype(jnp.float32)
    center = values - jnp.mean(values, -1, keepdims=True)
    spread = lax.rsqrt(jnp.mean(center * center, -1, keepdims=True) + epsilon)
    scaled = center * spread
    return (scaled, spread, (scaled * norm_gain).astype(jnp.bfloat16))


def attend_backward(queries, key_rows, values, upstream, allowed, factor):
    scores = (
        lax.dot_general(
            queries, key_rows, (((1,), (1,)), ((), ())), preferred_element_type=jnp.float32
        )
        * factor
    )
    scores = jnp.where(allowed, scores, masked)
    powers = jnp.exp(scores - jnp.max(scores, -1, keepdims=True))
    weights = powers / jnp.sum(powers, -1, keepdims=True)
    rounded = weights.astype(jnp.bfloat16)
    output = jnp.dot(rounded, values, preferred_element_type=jnp.float32)
    center_term = jnp.sum(upstream.astype(jnp.float32) * output, -1, keepdims=True)
    grad_values = lax.dot_general(
        rounded, upstream, (((0,), (0,)), ((), ())), preferred_element_type=jnp.float32
    ).astype(jnp.bfloat16)
    grad_weights = lax.dot_general(
        upstream, values, (((1,), (1,)), ((), ())), preferred_element_type=jnp.float32
    )
    grad_scores = (weights * (grad_weights - center_term) * factor).astype(jnp.bfloat16)
    grad_queries = jnp.dot(grad_scores, key_rows, preferred_element_type=jnp.float32).astype(
        jnp.bfloat16
    )
    grad_keys = lax.dot_general(
        grad_scores, queries, (((0,), (0,)), ((), ())), preferred_element_type=jnp.float32
    ).astype(jnp.bfloat16)
    return (grad_queries, grad_keys, grad_values)


def cluster_grads(payload, validity, head_width):
    row_count = payload.shape[0]
    spans = payload.shape[1] // 4
    heads_local = spans // head_width
    positions = lax.broadcasted_iota(jnp.int32, (row_count, row_count), 0)
    others = lax.broadcasted_iota(jnp.int32, (row_count, row_count), 1)
    allowed = (positions >= others) & (validity[None, :] > 0)
    factor = head_width ** (-0.5)

    def one_head(head_index, result):
        offset = head_index * head_width

        def select(portion):
            return lax.dynamic_slice_in_dim(payload, portion * spans + offset, head_width, 1)

        grads_head = attend_backward(select(0), select(1), select(2), select(3), allowed, factor)
        for portion in range(3):
            result = lax.dynamic_update_slice_in_dim(
                result, grads_head[portion], portion * spans + offset, 1
            )
        return result

    return lax.fori_loop(0, heads_local, one_head, jnp.zeros((row_count, 3 * spans), jnp.bfloat16))


def on_device(hidden, norm_gain, projection, upstream, cluster):
    seq_count = lax.axis_size("seq")
    tokens = hidden.shape[1]
    width_model = hidden.shape[2]
    spans = projection.shape[2]
    clusters_all = CLUS_DEV * seq_count
    slot_rows = 3 * tokens // clusters_all
    scaled, spread, normed = normalize(hidden[0], norm_gain)
    labels = cluster[0, :, 0]
    member = (labels[:, None] == jnp.arange(clusters_all, dtype=jnp.int32)[None, :]).astype(
        jnp.int32
    )
    ranks = jnp.sum(jnp.cumsum(member, 0) * member, 1) - 1
    target = labels * slot_rows + ranks
    projected = jnp.einsum(
        "td,kdh->tkh", normed, projection, preferred_element_type=jnp.float32
    ).astype(jnp.bfloat16)
    payload = jnp.concatenate([projected.reshape(tokens, 3 * spans), upstream[0]], 1)
    columns = payload.shape[1]
    outgoing = jnp.zeros((clusters_all * slot_rows, columns), jnp.bfloat16).at[target].set(payload)
    outgoing = outgoing.reshape(seq_count, CLUS_DEV, slot_rows, columns)
    present = jnp.zeros((clusters_all * slot_rows,), jnp.bfloat16).at[target].set(1.0)
    present = present.reshape(seq_count, CLUS_DEV, slot_rows)
    rows_in = lax.all_to_all(outgoing, "seq", split_axis=0, concat_axis=0, tiled=True)
    marks_in = lax.all_to_all(present, "seq", split_axis=0, concat_axis=0, tiled=True)
    sources = rows_in.shape[0]
    item_count = rows_in.shape[1]
    stacked = jnp.swapaxes(rows_in, 0, 1).reshape(item_count, sources * slot_rows, rows_in.shape[3])
    mark_rows = jnp.swapaxes(marks_in, 0, 1).reshape(item_count, sources * slot_rows)

    def per_item(entries):
        return cluster_grads(entries[0], entries[1].astype(jnp.float32), HDIM)

    results = lax.map(per_item, (stacked, mark_rows))
    width_out = results.shape[-1]
    results = results.reshape(item_count, sources, slot_rows, width_out)
    answer = jnp.swapaxes(results, 0, 1)
    returned = lax.all_to_all(answer, "seq", split_axis=0, concat_axis=0, tiled=True)
    restored = returned.reshape(clusters_all * slot_rows, 3 * spans)[target]
    partial_value = jnp.einsum(
        "tkh,kdh->td",
        restored.reshape(tokens, 3, spans),
        projection,
        preferred_element_type=jnp.float32,
    )
    partial_value = lax.optimization_barrier(partial_value.astype(jnp.bfloat16)).astype(jnp.float32)
    half_width = width_model // lax.axis_size("head")
    offset = lax.axis_index("head") * half_width
    own_scaled = lax.dynamic_slice_in_dim(scaled, offset, half_width, 1)
    own_gain = lax.dynamic_slice_in_dim(norm_gain, offset, half_width, 0)
    gradient = lax.psum_scatter(
        partial_value.astype(jnp.bfloat16), "head", scatter_dimension=1, tiled=True
    ).astype(jnp.float32)
    scaled_grad = gradient * own_gain
    first_sum, second_sum = lax.psum(
        (
            jnp.sum(scaled_grad, -1, keepdims=True),
            jnp.sum(scaled_grad * own_scaled, -1, keepdims=True),
        ),
        "head",
    )
    first_mean = first_sum / width_model
    second_mean = second_sum / width_model
    input_gradient = (spread * (scaled_grad - first_mean - own_scaled * second_mean)).astype(
        jnp.bfloat16
    )
    local_sum = jnp.sum(gradient * own_scaled, 0)
    gain_total = lax.psum(local_sum, ("seq", "dp"))
    gain_gradient = gain_total * (seq_count * lax.axis_size("dp") * tokens) ** (-0.5)
    return (input_gradient.reshape(1, tokens, half_width), gain_gradient)


def solution(mesh):
    in_specs = (
        P("dp", "seq", None),
        P(),
        P(None, None, "head"),
        P("dp", "seq", "head"),
        P("dp", "seq", None),
    )
    out_specs = (P("dp", "seq", "head"), P("head"))
    return jax.shard_map(
        on_device, mesh=mesh, in_specs=in_specs, out_specs=out_specs, check_vma=False
    )
```

profile of v0, /device:TPU:1, one launch (start us, length us, event | category | flops | bytes accessed | tf_op | source)
XLA Modules:
  0.0 1259.5 jit_solution(10916248163489631353)
XLA Ops:
  12.9 19.1 %all-to-all-start.1 = ((bf16[64,1,9]{2,1,0:T(2,128)(2,1)}), bf16[64,1,9]{2,1,0:T(2,128)(2,1)S(1)}, u32[]{:S(2)}, u32[]{:S(2)}) async-start(bf16[64,1,9]{2,1,0:T(2,128)(2,1)} %reshape.133), calls=%async_computation.1 | async-start | bytes 65536 | tf_op jit(solution)/shard_map/all_to_all | solution.py:100
  37.2 4.1 scatter_custom_fusion
  41.3 4.6 reshape.101
  45.9 14.8 %all-to-all-start = ((bf16[64,1,9,2048]{3,2,1,0:T(8,128)(2,1)}), bf16[64,1,9,2048]{3,2,1,0:T(8,128)(2,1)}, u32[]{:S(2)}, u32[]{:S(2)}) async-start(bf16[64,1,9,2048]{3,2,1,0:T(8,128)(2,1)} %bitcast.69), calls=%async_computation | async-start | bytes 8388608 | tf_op jit(solution)/shard_map/all_to_all | solution.py:99
  61.0 183.4 %all-to-all-done = bf16[64,1,9,2048]{3,2,1,0:T(8,128)(2,1)} async-done(((bf16[64,1,9,2048]{3,2,1,0:T(8,128)(2,1)}), bf16[64,1,9,2048]{3,2,1,0:T(8,128)(2,1)}, u32[]{:S(2)}, u32[]{:S(2)}) %all-to-all-start) | async-done | bytes 2359328 | tf_op jit(solution)/shard_map/all_to_all | solution.py:99
  244.3 4.7 squeeze.14
  249.0 4.3 copy.24
  254.8 113.3 %while.24 = (s32[]{:T(128)}, bf16[576,1536]{0,1:T(8,128)(2,1)}, bf16[576,2048]{0,1:T(8,128)(2,1)}, pred[576]{0:T(1024)(128)(4,1)S(1)}, s32[]{:T(128)}, /*index=5...) while((s32[]{:T(128)}, bf16[576,1536]{0,1:T(8,128)(2,1)}, ...), condition=%wide.region_11.12_spmd.clone, body=%wide.region_7.11_spmd.clone.sunk | while | flops 260331856 | bytes 16045296 | solution.py:73
  259.8 2.9 multiply_convert_fusion.3
  274.0 2.9 multiply_convert_fusion.3
  281.0 2.1 fusion.93
  288.2 2.9 multiply_convert_fusion.3
  293.1 2.1 fusion.92
  302.3 2.9 multiply_convert_fusion.3
  309.4 2.1 fusion.93
  316.5 2.9 multiply_convert_fusion.3
  330.7 2.9 multiply_convert_fusion.3
  344.8 2.9 multiply_convert_fusion.3
  349.7 2.1 fusion.92
  359.0 2.9 multiply_convert_fusion.3
  363.9 2.1 fusion.92
  366.0 2.1 fusion.93
  368.1 3.9 copy.25
  372.0 4.2 transpose_reshape.3
  376.2 11.6 all-to-all-start.2
  388.1 137.9 %all-to-all-done.2 = bf16[64,1,9,1536]{3,2,1,0:T(8,128)(2,1)} async-done(((bf16[64,1,9,1536]{3,2,1,0:T(8,128)(2,1)}), bf16[64,1,9,1536]{3,2,1,0:T(8,128)(2,1)}, u32[]{:S(2)}, u32[]{:S(2)}) %all-to-all-start.2) | async-done | bytes 1769504 | tf_op jit(solution)/shard_map/all_to_all | solution.py:113
  526.0 4.2 reshape.103
  530.2 4.1 gather_fusion
  534.4 3.0 fusion.24
  538.6 17.6 %reduce-scatter.2.cloned.1.call-done = bf16[192,512]{1,0:T(8,128)(2,1)} async-done(((bf16[192,1024]{1,0:T(8,128)(2,1)}), bf16[192,512]{1,0:T(8,128)(2,1)}) %reduce-scatter.2.cloned.1.call-update) | async-done | bytes 196624 | tf_op jit(solution)/shard_map/reduce_scatter | solution.py:126
  557.6 579.8 %psum.23 = f32[512]{0:T(512)S(1)} all-reduce(f32[512]{0:T(512)S(1)} %get-tuple-element.173), channel_id=1, replica_groups=mesh['seq'=64,'head'=2,'dp'=4] {'seq','dp'}, use_global_device_ids=true, to_apply=%region_18.19 | all-reduce | flops 512 | bytes 4096 | tf_op jit(solution)/shard_map/psum | solution.py:143
  1138.0 112.8 %all-reduce.1 = (f32[192,1]{0,1:T(1,128)S(1)}, f32[192,1]{0,1:T(1,128)S(1)}) all-reduce(f32[192,1]{0,1:T(1,128)S(1)} %bitcast.76, f32[192,1]{0,1:T(1,128)S(1)} %bitcast.77), channel_id=1, replica_groups=mesh['seq'=64,'head'=2,'dp'=4] {'head'}, use_global_device_ids=true, to_apply=%region_16.17 | all-reduce | flops 384 | bytes 3072 | tf_op jit(solution)/shard_map/psum | solution.py:130
  (106 shorter events, 95.4 us)
Async XLA Ops:
  7.2 27.3 %copy-start = (bf16[3,1024,512]{2,1,0:T(8,128)(2,1)S(1)}, bf16[3,1024,512]{2,1,0:T(8,128)(2,1)}, u32[]{:S(2)}) copy-start(bf16[3,1024,512]{2,1,0:T(8,128)(2,1)} %param.9) | copy-start | bytes 9437188
  12.9 33.0 %all-to-all-start.1 = ((bf16[64,1,9]{2,1,0:T(2,128)(2,1)}), bf16[64,1,9]{2,1,0:T(2,128)(2,1)S(1)}, u32[]{:S(2)}, u32[]{:S(2)}) async-start(bf16[64,1,9]{2,1,0:T(2,128)(2,1)} %reshape.133), calls=%async_computation.1 | async-start | bytes 65536 | tf_op jit(solution)/shard_map/all_to_all | solution.py:100
  34.4 2.8 copy-start.3
  45.9 198.5 %all-to-all-start = ((bf16[64,1,9,2048]{3,2,1,0:T(8,128)(2,1)}), bf16[64,1,9,2048]{3,2,1,0:T(8,128)(2,1)}, u32[]{:S(2)}, u32[]{:S(2)}) async-start(bf16[64,1,9,2048]{3,2,1,0:T(8,128)(2,1)} %bitcast.69), calls=%async_computation | async-start | bytes 8388608 | tf_op jit(solution)/shard_map/all_to_all | solution.py:99
  256.1 1.2 copy-start.1
  270.3 1.2 copy-start.1
  284.5 1.2 copy-start.1
  298.7 1.2 copy-start.1
  312.8 1.2 copy-start.1
  327.0 1.2 copy-start.1
  341.1 1.2 copy-start.1
  355.3 1.2 copy-start.1
  376.2 149.7 %all-to-all-start.2 = ((bf16[64,1,9,1536]{3,2,1,0:T(8,128)(2,1)}), bf16[64,1,9,1536]{3,2,1,0:T(8,128)(2,1)}, u32[]{:S(2)}, u32[]{:S(2)}) async-start(bf16[64,1,9,1536]{3,2,1,0:T(8,128)(2,1)} %bitcast.70), calls=%async_computation.2 | async-start | bytes 6291456 | tf_op jit(solution)/shard_map/all_to_all | solution.py:113
  387.8 168.4 %reduce-scatter.2.cloned.1.call-start = ((), (), s32[]{:S(2)}) async-start(), calls=%async_computation.4 | async-start | bytes 589824 | tf_op jit(solution)/shard_map/reduce_scatter | solution.py:126
  534.4 3.1 copy-start.4
  534.4 3.1 copy-start.2
Sparse Core Ops, SparseCore 0:
  537.5 18.6 reduce-scatter.1
where the time goes:
time: 1260 us
  blocking collectives  693 us (55%)
  waiting for transfers between devices  339 us (27%)
  matrix products  99.9 us (8%)
  starting transfers between devices  45.7 us (4%)
  local copies, waits for them, and re-layouts  42.7 us (3%)
  other arithmetic  25.4 us (2%)
  between operations  14.2 us (1%)
    psum x1, blocking collectives, on_device(): gain_total = lax.psum(local_sum, ('seq', 'dp'))  580 us
    all_to_all x1, waiting for transfers between devices, on_device(): lax.all_to_all(outgoing, 'seq', split_axis=0, concat_axis=0, tiled=True)  183 us
    all_to_all x1, waiting for transfers between devices, on_device(): lax.all_to_all(answer, 'seq', split_axis=0, concat_axis=0, tiled=True)  138 us
    psum x1, blocking collectives, on_device(): lax.psum((jnp.sum(scaled_grad, -1, keepdims=True), jnp.sum(scaled_grad *...  113 us
  transfers between devices with their start and end apart: 4, of which 3 were waited for; matrix products, arithmetic and copies ran while one was open for 1% of the time, Pallas kernels for 0%

commit v1 on v0

v1 whole, which is shorter than its diff:
```python
import jax
import jax.numpy as jnp
from jax import lax
from jax.experimental import pallas as pl
from jax.experimental.pallas import tpu as pltpu
from jax.sharding import PartitionSpec as P

HDIM = 64
EPSILON = 1e-05
MASKED = -1e30
PAD_MARK = 64.0
f32 = jnp.float32
bf16 = jnp.bfloat16


def dims(lhs, rhs, left, right):
    return lax.dot_general(lhs, rhs, (((left,), (right,)), ((), ())), preferred_element_type=f32)


def iota(shape, dim):
    return lax.broadcasted_iota(jnp.int32, shape, dim)


def vmem_call(kernel, out_shape, scratch=(), limit=56, scalars=0, count=1):
    spec = pl.BlockSpec(memory_space=pltpu.VMEM)
    return pl.pallas_call(
        kernel,
        out_shape=out_shape,
        in_specs=[pl.BlockSpec(memory_space=pltpu.SMEM)] * scalars + [spec] * count,
        out_specs=jax.tree.map(lambda _: spec, out_shape),
        scratch_shapes=scratch,
        compiler_params=pltpu.CompilerParams(vmem_limit_bytes=limit * 2**20),
    )


def pack_kernel(slots, head_ref, hidden_ref, gain_ref, up_ref, lab_ref, labrow_ref, out_ref, spread_ref):
    tokens, width = hidden_ref.shape
    half = width // 2
    x = hidden_ref[...].astype(f32)
    center = x - jnp.mean(x, -1, keepdims=True)
    spread = lax.rsqrt(jnp.mean(center * center, -1, keepdims=True) + EPSILON)
    spread_ref[...] = spread
    normed = (center * spread * gain_ref[...]).astype(bf16)
    own = jnp.where(head_ref[0] == 0, normed[:, :half], normed[:, half:])
    up = up_ref[...]
    lab, labrow = lab_ref[...], labrow_ref[...]
    before = (lab == labrow) & (iota((tokens, tokens), 0) < iota((tokens, tokens), 1))
    rank = jnp.sum(before.astype(f32), 0, keepdims=True).astype(jnp.int32)
    rows = out_ref.shape[0]
    key = jnp.where(rank < slots - 1, labrow * 8 + rank, -1)
    last = jnp.where(rank == slots - 1, labrow, -1)
    row = iota((rows, tokens), 0)
    hot = (row == key).astype(f32)
    taken = jnp.sum(hot, -1, keepdims=True)
    hot = hot.astype(bf16)
    out_ref[:, :half] = dims(hot, own, 1, 0).astype(bf16)
    right = dims(hot, up, 1, 0)
    first = iota((rows, half), 1) == 0
    out_ref[:, half:width] = jnp.where(first & (taken == 0), PAD_MARK, right).astype(bf16)
    hot_last = ((row >> 3) == last).astype(f32)
    taken = jnp.sum(hot_last, -1, keepdims=True)
    piece = iota((rows, tokens), 0) & 7
    total = jnp.zeros((rows, 128), f32)
    for i in range(8):
        source = (own if i < 4 else up)[:, (i % 4) * 128 : (i % 4 + 1) * 128]
        total = total + dims(jnp.where(piece == i, hot_last, 0.0).astype(bf16), source, 1, 0)
    mark = (iota((rows, 128), 1) == 0) & ((iota((rows, 128), 0) & 7) == 4) & (taken == 0)
    out_ref[:, width:] = jnp.where(mark, PAD_MARK, total).astype(bf16)


def attend_kernel(head_ref, recv_ref, other_ref, weights_ref, gain_ref, part_ref, sums_ref,
                  x_ref, u_ref, q_ref, k_ref, v_ref, g_ref, dq_ref):
    rows, extended = recv_ref.shape
    half = weights_ref.shape[2]
    width = 2 * half
    sources = rows // 8
    total = rows + sources
    head = head_ref[0]
    pick_col, pick_row = iota((sources, rows), 1), iota((sources, rows), 0)

    def ninth(ref, i):
        pick = (pick_col == pick_row * 8 + i).astype(bf16)
        return dims(pick, ref[:, width:], 1, 0).astype(bf16)

    x_ref[0, :rows, :] = recv_ref[:, :half]
    x_ref[1, :rows, :] = other_ref[:, :half]
    u_ref[:rows, :] = recv_ref[:, half:width]
    for i in range(4):
        span = slice(i * 128, (i + 1) * 128)
        x_ref[0, rows:, span] = ninth(recv_ref, i)
        x_ref[1, rows:, span] = ninth(other_ref, i)
        u_ref[rows:, span] = ninth(recv_ref, 4 + i)
    up = u_ref[:, :128]
    pads = up[:, :1].astype(f32) > 0.5 * PAD_MARK
    u_ref[:, :128] = jnp.where(pads & (iota((total, 128), 1) == 0), 0.0, up.astype(f32)).astype(bf16)
    own_rows = pl.ds(pl.multiple_of(head * half, half), half)
    other_rows = pl.ds(pl.multiple_of((1 - head) * half, half), half)
    own, other = x_ref[0], x_ref[1]
    for n, ref in enumerate((q_ref, k_ref, v_ref)):
        ref[...] = (
            dims(own, weights_ref[n, own_rows, :], 1, 0) + dims(other, weights_ref[n, other_rows, :], 1, 0)
        ).astype(bf16)

    def order(i):
        return jnp.where(i < rows, (i >> 3) * 9 + (i & 7), (i - rows) * 9 + 8)

    factor = HDIM**-0.5
    place = jnp.where(pads, 2 * total, order(iota((total, 1), 0)))
    allowed = place <= order(iota((1, total), 1))
    left = iota((total, 128), 1) < HDIM

    def pair(p, carry):
        span = pl.ds(pl.multiple_of(p * 128, 128), 128)
        q, k, v, u = q_ref[:, span], k_ref[:, span], v_ref[:, span], u_ref[:, span]
        made = []
        for side in (left, ~left):
            ks = jnp.where(side, k, 0).astype(bf16)
            vs = jnp.where(side, v, 0).astype(bf16)
            scores = jnp.where(allowed, dims(ks, q, 1, 1) * factor, MASKED)
            powers = jnp.exp(scores - jnp.max(scores, 0, keepdims=True))
            weights = powers / jnp.sum(powers, 0, keepdims=True)
            rounded = weights.astype(bf16)
            grads = dims(vs, u, 1, 1)
            center = jnp.sum(rounded.astype(f32) * grads, 0, keepdims=True)
            ds = (weights * (grads - center) * factor).astype(bf16)
            made.append((dims(rounded, u, 1, 0), dims(ds, q, 1, 0), dims(ks, ds, 0, 0)))
        (gv0, gk0, gq0), (gv1, gk1, gq1) = made
        g_ref[0, :, span] = jnp.where(left, gk0, gk1).astype(bf16)
        g_ref[1, :, span] = jnp.where(left, gv0, gv1).astype(bf16)
        dq_ref[span, :] = (gq0 + gq1).astype(bf16)
        return carry

    lax.fori_loop(0, half // 128, pair, 0)
    for c in range(2):
        lines = slice(c * half, (c + 1) * half)
        partial = (
            dims(dq_ref[...], weights_ref[0, lines, :], 0, 1)
            + dims(g_ref[0], weights_ref[1, lines, :], 1, 1)
            + dims(g_ref[1], weights_ref[2, lines, :], 1, 1)
        ).astype(bf16)
        part_ref[:, lines] = partial
        normed = x_ref[jnp.where(head == c, 0, 1)].astype(f32)
        sums_ref[:, lines] = jnp.sum(partial.astype(f32) * normed, 0, keepdims=True) / gain_ref[:, lines]


def combine_kernel(head_ref, part_ref, other_ref, recv_ref, peer_ref, gain_ref, out_ref):
    rows = recv_ref.shape[0]
    total, width = part_ref.shape
    half = width // 2
    sources = rows // 8
    head = head_ref[0]
    pick_col, pick_row = iota((sources, rows), 1), iota((sources, rows), 0)

    def tokens_of(ref):
        pieces = [
            dims((pick_col == pick_row * 8 + i).astype(bf16), ref[:, width:], 1, 0) for i in range(4)
        ]
        return jnp.concatenate([ref[:, :half].astype(f32), jnp.concatenate(pieces, 1)], 0)

    own, peer = tokens_of(recv_ref), tokens_of(peer_ref)
    gain = gain_ref[...]

    def pick_half(array, own_half):
        return jnp.where((head == 0) == own_half, array[:, :half], array[:, half:])

    grad = part_ref[...].astype(f32) + other_ref[...].astype(f32)
    grad_own, grad_peer = pick_half(grad, True), pick_half(grad, False)
    gain_own, gain_peer = pick_half(gain, True), pick_half(gain, False)
    first = (jnp.sum(grad_own * gain_own, -1, keepdims=True) + jnp.sum(grad_peer * gain_peer, -1, keepdims=True)) / width
    second = (jnp.sum(grad_own * own, -1, keepdims=True) + jnp.sum(grad_peer * peer, -1, keepdims=True)) / width
    result = (grad_own * gain_own - first - own / gain_own * second).astype(bf16)
    out_ref[:, :half] = result[:rows]
    ext = jnp.zeros((rows, 128), f32)
    put_row, put_col = iota((rows, sources), 0), iota((rows, sources), 1)
    for i in range(4):
        put = (put_row == put_col * 8 + i).astype(bf16)
        ext = ext + dims(put, result[rows:, i * 128 : (i + 1) * 128], 1, 0)
    out_ref[:, half:] = ext.astype(bf16)


def finish_kernel(slots, back_ref, lab_ref, labrow_ref, spread_ref, out_ref):
    tokens, half = out_ref.shape
    rows = back_ref.shape[0]
    lab, labrow = lab_ref[...], labrow_ref[...]
    before = (lab == labrow) & (iota((tokens, tokens), 1) < iota((tokens, tokens), 0))
    rank = jnp.sum(before.astype(f32), -1, keepdims=True).astype(jnp.int32)
    key = jnp.where(rank < slots - 1, lab * 8 + rank, -1)
    last = jnp.where(rank == slots - 1, lab, -1)
    col = iota((tokens, rows), 1)
    hot = (col == key).astype(bf16)
    hot_last = (col >> 3) == last
    spread = spread_ref[...]
    for i in range(half // 128):
        span = slice(i * 128, (i + 1) * 128)
        value = dims(hot, back_ref[:, span], 1, 0)
        value = value + dims((hot_last & ((col & 7) == i)).astype(bf16), back_ref[:, half:], 1, 0)
        out_ref[:, span] = (value * spread).astype(bf16)


def on_device(hidden, norm_gain, projection, upstream, cluster):
    sources = lax.axis_size("seq")
    tokens, width = hidden.shape[1:]
    half = projection.shape[2]
    slots = 3 * tokens // sources
    total, rows = sources * slots, sources * 8
    head = lax.axis_index("head").astype(jnp.int32).reshape(1)
    gain = norm_gain.reshape(1, width)
    lab = cluster[0]
    labrow = lab.reshape(1, tokens)
    shape = jax.ShapeDtypeStruct
    swap = [(0, 1), (1, 0)]

    sent, spread = vmem_call(
        lambda *refs: pack_kernel(slots, *refs),
        (shape((rows, width + 128), bf16), shape((tokens, 1), f32)),
        scalars=1,
        count=5,
    )(head, hidden[0], gain, upstream[0], lab, labrow)
    recv = lax.all_to_all(sent.reshape(sources, 8, width + 128), "seq", 0, 0, tiled=True)
    recv = recv.reshape(rows, width + 128)
    peer = lax.ppermute(recv, "head", swap)
    part, sums = vmem_call(
        attend_kernel,
        (shape((total, width), bf16), shape((1, width), f32)),
        scratch=[
            pltpu.VMEM((2, total, half), bf16),
            pltpu.VMEM((total, half), bf16),
            pltpu.VMEM((total, half), bf16),
            pltpu.VMEM((total, half), bf16),
            pltpu.VMEM((total, half), bf16),
            pltpu.VMEM((2, total, half), bf16),
            pltpu.VMEM((half, total), bf16),
        ],
        scalars=1,
        count=4,
    )(head, recv, peer, projection, gain)
    other = lax.ppermute(part, "head", swap)
    answer = vmem_call(combine_kernel, shape((rows, half + 128), bf16), scalars=1, count=5)(
        head, part, other, recv, peer, gain
    )
    back = lax.all_to_all(answer.reshape(sources, 8, half + 128), "seq", 0, 0, tiled=True)
    back = back.reshape(rows, half + 128)
    side = sources // 16 if sources % 16 == 0 else 1
    across = [[z * side + x for x in range(side)] for z in range(sources // side)]
    along = [[z * side + x for z in range(sources // side)] for x in range(side)]
    gain_sum = lax.psum(sums.reshape(width), ("dp", "head"))
    gain_sum = lax.psum(gain_sum, "seq", axis_index_groups=across)
    gain_sum = lax.psum(gain_sum, "seq", axis_index_groups=along)
    gain_sum = lax.dynamic_slice_in_dim(gain_sum, head[0] * half, half, 0)
    gain_gradient = gain_sum * (sources * lax.axis_size("dp") * tokens) ** (-0.5)
    result = vmem_call(lambda *refs: finish_kernel(slots, *refs), shape((tokens, half), bf16), count=4)(
        back, lab, labrow, spread
    )
    return (result.reshape(1, tokens, half), gain_gradient)


def solution(mesh):
    in_specs = (
        P("dp", "seq", None),
        P(),
        P(None, None, "head"),
        P("dp", "seq", "head"),
        P("dp", "seq", None),
    )
    out_specs = (P("dp", "seq", "head"), P("head"))
    return jax.shard_map(
        on_device, mesh=mesh, in_specs=in_specs, out_specs=out_specs, check_vma=False
    )
```

time: 1260 us -> 187 us (0.15)
  the two profiles are of different devices: /device:TPU:1 before, /device:TPU:32 now
where the time goes in v1:
time: 187 us
  blocking collectives  133 us (71%)
  Pallas kernels  31.3 us (17%)
  starting transfers between devices  11.1 us (6%)
  waiting for transfers between devices  5.71 us (3%)
  local copies, waits for them, and re-layouts  4.37 us (2%)
    all_to_all x1, blocking collectives, on_device(): lax.all_to_all(sent.reshape(sources, 8, width + 128), 'seq', 0, 0, tiled=...  77.9 us
    psum x1, blocking collectives, on_device(): gain_sum = lax.psum(gain_sum, 'seq', axis_index_groups=along)  29.3 us
    pallas_call x1, Pallas kernels, on_device(): vmem_call(attend_kernel, (shape((total, width), bf16), shape((1, width),...  20.7 us
    psum x1, blocking collectives, on_device(): gain_sum = lax.psum(sums.reshape(width), ('dp', 'head'))  14.6 us
    psum x1, blocking collectives, on_device(): gain_sum = lax.psum(gain_sum, 'seq', axis_index_groups=across)  11 us
    all_to_all x1, starting transfers between devices, on_device(): lax.all_to_all(answer.reshape(sources, 8, half + 128), 'seq', 0, 0, tiled...  7.15 us
    pallas_call x1, Pallas kernels, on_device(): vmem_call(combine_kernel, shape((rows, half + 128), bf16), scalars=1, cou...  4.41 us
  transfers between devices with their start and end apart: 3, of which 2 were waited for; matrix products, arithmetic and copies ran while one was open for 0% of the time, Pallas kernels for 0%

profile of v1, /device:TPU:32, one launch (start us, length us, event | category | flops | bytes accessed | tf_op | source)
XLA Modules:
  0.0 186.7 jit_solution(12598846899073828065)
XLA Ops:
  0.6 1.4 copy.7.refs_4_.refs_1_
  2.1 3.5 %shard_map.68 = (bf16[512,1152]{1,0:T(8,128)(2,1)}, f32[192,1]{1,0:T(8,128)}) custom-call(s32[1]{0:T(128)} %bitcast.refs_0_.head_ref, bf16[192,1024]{1,0:T(8,128)(2,1)} %bitcast.18, f32[1,1024]{1,0:T(1,128)} %bitcast.21, bf16[192,512]{1,0:T(8,128)(2,1)} %bitcast.20, s32[192,1]{1,0:T(8,128)} %copy.7.refs_4_.refs_1_, s32[1,192]{1,0:T(1,128)} %bitcast.25), custom_call_target="tpu_custom_call" | custom-call | tf_op jit(solution)/shard_map/pallas_call | solution.py:213
  5.6 77.9 %all_to_all.10 = bf16[64,8,1152]{2,1,0:T(8,128)(2,1)S(1)} all-to-all(bf16[64,8,1152]{2,1,0:T(8,128)(2,1)} %bitcast.17), channel_id=1, replica_groups=mesh['seq'=64,'head'=2,'dp'=4] {'seq'}, dimensions={0} | all-to-all | bytes 2359296 | tf_op jit(solution)/shard_map/all_to_all | solution.py:219
  83.5 0.0 copy-start
  83.5 1.9 %collective-permute-start = (bf16[512,1152]{1,0:T(8,128)(2,1)S(1)}, bf16[512,1152]{1,0:T(8,128)(2,1)S(1)}, u32[]{:S(2)}, u32[]{:S(2)}) collective-permute-start(bf16[512,1152]{1,0:T(8,128)(2,1)S(1)} %bitcast.12), channel_id=1, source_target_pairs={{0,4},{4,0},{1,5},{5,1},{2,6},{6,2},{3,7},{7,3},{8,12},{12,8},{9,1... | collective-permute-start | bytes 3538952 | tf_op jit(solution)/shard_map/ppermute | solution.py:221
  85.5 2.8 %collective-permute-done.other_ref.peer_ref = bf16[512,1152]{1,0:T(8,128)(2,1)S(1)} collective-permute-done((bf16[512,1152]{1,0:T(8,128)(2,1)S(1)}, bf16[512,1152]{1,0:T(8,128)(2,1)S(1)}, u32[]{:S(2)}, u32[]{:S(2)}) %collective-permute-start) | collective-permute-done | bytes 1179680 | tf_op jit(solution)/shard_map/ppermute | solution.py:221
  88.3 0.0 copy-done
  88.3 0.0 copy-start.1
  88.3 1.1 copy-done.1
  89.3 20.7 %shard_map.69 = (bf16[576,1024]{1,0:T(8,128)(2,1)}, f32[1,1024]{1,0:T(1,128)}) custom-call(s32[1]{0:T(128)} %bitcast.refs_0_.head_ref, bf16[512,1152]{1,0:T(8,128)(2,1)} %bitcast.13, bf16[512,1152]{1,0:T(8,128)(2,1)} %copy-done.1, bf16[3,1024,512]{2,1,0:T(8,128)(2,1)} %weights_ref.1, f32[1,1024]{1,0:T(1,128)} %bitcast.22), custom_call_target="tpu_custom_call" | custom-call | tf_op jit(solution)/shard_map/pallas_call | solution.py:222
  110.1 2.0 %collective-permute-start.1 = (bf16[576,1024]{1,0:T(8,128)(2,1)}, bf16[576,1024]{1,0:T(8,128)(2,1)S(1)}, u32[]{:S(2)}, u32[]{:S(2)}) collective-permute-start(bf16[576,1024]{1,0:T(8,128)(2,1)} %get-tuple-element.7.part_ref), channel_id=1, source_target_pairs={{0,4},{4,0},{1,5},{5,1},{2,6},{6,2},{3,7},{7,3},{8,12},{12,8},{9,1... | collective-permute-start | bytes 3538952 | tf_op jit(solution)/shard_map/ppermute | solution.py:237
  112.1 2.9 %collective-permute-done.1.other_ref = bf16[576,1024]{1,0:T(8,128)(2,1)S(1)} collective-permute-done((bf16[576,1024]{1,0:T(8,128)(2,1)}, bf16[576,1024]{1,0:T(8,128)(2,1)S(1)}, u32[]{:S(2)}, u32[]{:S(2)}) %collective-permute-start.1) | collective-permute-done | bytes 1179680 | tf_op jit(solution)/shard_map/ppermute | solution.py:237
  115.0 0.0 copy-start.3
  115.0 1.0 copy-done.3
  116.0 4.4 %shard_map.70 = bf16[512,640]{1,0:T(8,128)(2,1)} custom-call(s32[1]{0:T(128)} %bitcast.refs_0_.head_ref, bf16[576,1024]{1,0:T(8,128)(2,1)} %get-tuple-element.7.part_ref, bf16[576,1024]{1,0:T(8,128)(2,1)} %copy-done.3, bf16[512,1152]{1,0:T(8,128)(2,1)} %bitcast.14, bf16[512,1152]{1,0:T(8,128)(2,1)} %copy-done.1, f32[1,1024]{1,0:T(1,128)} %bitcast.23), custom_call_target="tpu_custom_call" | custom-call | tf_op jit(solution)/shard_map/pallas_call | solution.py:238
  120.4 0.0 copy-start.4
  120.5 7.1 %all-to-all-start.1 = ((bf16[64,8,640]{2,1,0:T(8,128)(2,1)}), bf16[64,8,640]{2,1,0:T(8,128)(2,1)S(1)}, u32[]{:S(2)}, u32[]{:S(2)}) async-start(bf16[64,8,640]{2,1,0:T(8,128)(2,1)} %bitcast.15), calls=%async_computation.1 | async-start | bytes 1310720 | tf_op jit(solution)/shard_map/all_to_all | solution.py:241
  127.6 0.0 copy-done.4
  127.6 14.6 %psum.21 = f32[1024]{0:T(1024)S(1)} all-reduce(f32[1024]{0:T(1024)S(1)} %bitcast.27), channel_id=1, replica_groups=mesh['seq'=64,'head'=2,'dp'=4] {'dp','head'}, use_global_device_ids=true, to_apply=%region_0.0 | all-reduce | flops 1024 | bytes 8192 | tf_op jit(solution)/shard_map/psum | solution.py:246
  142.2 11.0 %psum.22 = f32[1024]{0:T(1024)S(1)} all-reduce(f32[1024]{0:T(1024)S(1)} %psum.21), channel_id=1, replica_groups={{0,8,16,24},{32,40,48,56},{64,72,80,88},{96,104,112,120},{128,136,144,1..., use_global_device_ids=true, to_apply=%region_1.0 | all-reduce | flops 1024 | bytes 8192 | tf_op jit(solution)/shard_map/psum | solution.py:247
  153.2 29.3 %psum.23 = f32[1024]{0:T(1024)S(1)} all-reduce(f32[1024]{0:T(1024)S(1)} %psum.22), channel_id=1, replica_groups={{0,32,64,96,128,160,192,224,256,288,320,352,384,416,448,480},{8,40,72,1..., use_global_device_ids=true, to_apply=%region_2.0 | all-reduce | flops 1024 | bytes 8192 | tf_op jit(solution)/shard_map/psum | solution.py:248
  182.5 0.7 dynamic-slice_multiply_fusion
  183.2 0.0 all-to-all-done.1
  183.2 0.0 copy-start.2
  183.2 0.8 copy-done.2
  184.0 2.7 %shard_map.71 = bf16[192,512]{1,0:T(8,128)(2,1)} custom-call(bf16[512,640]{1,0:T(8,128)(2,1)} %bitcast.16, s32[192,1]{1,0:T(8,128)} %copy.7.refs_4_.refs_1_, s32[1,192]{1,0:T(1,128)} %bitcast.26, f32[192,1]{1,0:T(8,128)} %get-tuple-element.8.refs_3_), custom_call_target="tpu_custom_call" | custom-call | tf_op jit(solution)/shard_map/pallas_call | solution.py:251
Async XLA Ops:
  83.5 4.7 %copy-start = (bf16[64,8,1152]{2,1,0:T(8,128)(2,1)}, bf16[64,8,1152]{2,1,0:T(8,128)(2,1)S(1)}, u32[]{:S(2)}) copy-start(bf16[64,8,1152]{2,1,0:T(8,128)(2,1)S(1)} %all_to_all.10) | copy-start | bytes 3538948
  83.5 4.7 %collective-permute-start = (bf16[512,1152]{1,0:T(8,128)(2,1)S(1)}, bf16[512,1152]{1,0:T(8,128)(2,1)S(1)}, u32[]{:S(2)}, u32[]{:S(2)}) collective-permute-start(bf16[512,1152]{1,0:T(8,128)(2,1)S(1)} %bitcast.12), channel_id=1, source_target_pairs={{0,4},{4,0},{1,5},{5,1},{2,6},{6,2},{3,7},{7,3},{8,12},{12,8},{9,1... | collective-permute-start | bytes 3538952 | tf_op jit(solution)/shard_map/ppermute | solution.py:221
  88.3 1.1 copy-start.1
  110.1 4.9 %collective-permute-start.1 = (bf16[576,1024]{1,0:T(8,128)(2,1)}, bf16[576,1024]{1,0:T(8,128)(2,1)S(1)}, u32[]{:S(2)}, u32[]{:S(2)}) collective-permute-start(bf16[576,1024]{1,0:T(8,128)(2,1)} %get-tuple-element.7.part_ref), channel_id=1, source_target_pairs={{0,4},{4,0},{1,5},{5,1},{2,6},{6,2},{3,7},{7,3},{8,12},{12,8},{9,1... | collective-permute-start | bytes 3538952 | tf_op jit(solution)/shard_map/ppermute | solution.py:237
  115.0 1.0 copy-start.3
  120.4 7.2 %copy-start.4 = (f32[1,1024]{1,0:T(1,128)S(1)}, f32[1,1024]{1,0:T(1,128)}, u32[]{:S(2)}) copy-start(f32[1,1024]{1,0:T(1,128)} %get-tuple-element.9) | copy-start | bytes 12292
  120.5 62.8 %all-to-all-start.1 = ((bf16[64,8,640]{2,1,0:T(8,128)(2,1)}), bf16[64,8,640]{2,1,0:T(8,128)(2,1)S(1)}, u32[]{:S(2)}, u32[]{:S(2)}) async-start(bf16[64,8,640]{2,1,0:T(8,128)(2,1)} %bitcast.15), calls=%async_computation.1 | async-start | bytes 1310720 | tf_op jit(solution)/shard_map/all_to_all | solution.py:241
  183.2 0.8 copy-start.2

commit v2 on v1

v2 whole, which is shorter than its diff:
```python
import jax
import jax.numpy as jnp
from jax import lax
from jax.experimental import pallas as pl
from jax.experimental.pallas import tpu as pltpu
from jax.sharding import PartitionSpec as P

HDIM = 64
EPSILON = 1e-05
MASKED = -1e30
PAD_MARK = 64.0
f32 = jnp.float32
bf16 = jnp.bfloat16


def dims(lhs, rhs, left, right):
    return lax.dot_general(lhs, rhs, (((left,), (right,)), ((), ())), preferred_element_type=f32)


def iota(shape, dim):
    return lax.broadcasted_iota(jnp.int32, shape, dim)


def vmem_call(kernel, out_shape, scratch=(), limit=8, scalars=0, count=1):
    spec = pl.BlockSpec(memory_space=pltpu.VMEM)
    return pl.pallas_call(
        kernel,
        out_shape=out_shape,
        in_specs=[pl.BlockSpec(memory_space=pltpu.SMEM)] * scalars + [spec] * count,
        out_specs=jax.tree.map(lambda _: spec, out_shape),
        scratch_shapes=scratch,
        compiler_params=pltpu.CompilerParams(vmem_limit_bytes=limit * 2**20),
    )


def column_of(labels):
    count = labels.shape[1]
    same = iota((count, count), 0) == iota((count, count), 1)
    return jnp.sum(jnp.where(same, labels.astype(f32), 0.0), -1, keepdims=True).astype(jnp.int32)


def pack_kernel(slots, head_ref, hidden_ref, gain_ref, up_ref, labrow_ref, out_ref, spread_ref):
    tokens, width = hidden_ref.shape
    half = width // 2
    x = hidden_ref[...].astype(f32)
    center = x - jnp.mean(x, -1, keepdims=True)
    spread = lax.rsqrt(jnp.mean(center * center, -1, keepdims=True) + EPSILON)
    spread_ref[...] = spread
    normed = (center * spread * gain_ref[...]).astype(bf16)
    own = jnp.where(head_ref[0] == 0, normed[:, :half], normed[:, half:])
    up = up_ref[...]
    labrow = labrow_ref[...]
    lab = column_of(labrow)
    before = (lab == labrow) & (iota((tokens, tokens), 0) < iota((tokens, tokens), 1))
    rank = jnp.sum(before.astype(f32), 0, keepdims=True).astype(jnp.int32)
    rows = out_ref.shape[0]
    key = jnp.where(rank < slots - 1, labrow * 8 + rank, -1)
    last = jnp.where(rank == slots - 1, labrow, -1)
    row = iota((rows, tokens), 0)
    hot = (row == key).astype(f32)
    taken = jnp.sum(hot, -1, keepdims=True)
    hot = hot.astype(bf16)
    out_ref[:, :half] = dims(hot, own, 1, 0).astype(bf16)
    right = dims(hot, up, 1, 0)
    first = iota((rows, half), 1) == 0
    out_ref[:, half:width] = jnp.where(first & (taken == 0), PAD_MARK, right).astype(bf16)
    hot_last = ((row >> 3) == last).astype(f32)
    taken = jnp.sum(hot_last, -1, keepdims=True)
    piece = iota((rows, tokens), 0) & 7
    total = jnp.zeros((rows, 128), f32)
    for i in range(8):
        source = (own if i < 4 else up)[:, (i % 4) * 128 : (i % 4 + 1) * 128]
        total = total + dims(jnp.where(piece == i, hot_last, 0.0).astype(bf16), source, 1, 0)
    mark = (iota((rows, 128), 1) == 0) & ((iota((rows, 128), 0) & 7) == 4) & (taken == 0)
    out_ref[:, width:] = jnp.where(mark, PAD_MARK, total).astype(bf16)


def thirds(value):
    high = value.astype(bf16)
    rest = value - high.astype(f32)
    middle = rest.astype(bf16)
    return high.astype(f32), middle.astype(f32), rest - middle.astype(f32)


def attend_kernel(head_ref, recv_ref, other_ref, weights_ref, gain_ref, keep_ref, send_ref, own_ref, stats_ref,
                  peer_ref, u_ref, q_ref, k_ref, v_ref, g_ref, dq_ref, bias_ref):
    rows, extended = recv_ref.shape
    half = weights_ref.shape[2]
    width = 2 * half
    late = rows // 8
    total = rows + late
    head = head_ref[0]
    pick_col, pick_row = iota((late, rows), 1), iota((late, rows), 0)
    own_ref[late:, :] = recv_ref[:, :half]
    peer_ref[late:, :] = other_ref[:, :half]
    u_ref[late:, :] = recv_ref[:, half:width]
    for i in range(4):
        span = slice(i * 128, (i + 1) * 128)
        pick = (pick_col == pick_row * 8 + i).astype(bf16)
        own_ref[:late, span] = dims(pick, recv_ref[:, width:], 1, 0).astype(bf16)
        peer_ref[:late, span] = dims(pick, other_ref[:, width:], 1, 0).astype(bf16)
        pick = (pick_col == pick_row * 8 + (i + 4)).astype(bf16)
        u_ref[:late, span] = dims(pick, recv_ref[:, width:], 1, 0).astype(bf16)
    up = u_ref[:, :128].astype(f32)
    pads = up[:, :1] > 0.5 * PAD_MARK
    u_ref[:, :128] = jnp.where(pads & (iota((total, 128), 1) == 0), 0.0, up).astype(bf16)
    own_rows = pl.ds(pl.multiple_of(head * half, half), half)
    other_rows = pl.ds(pl.multiple_of((1 - head) * half, half), half)
    own, peer = own_ref[...], peer_ref[...]
    factor = HDIM**-0.5
    for n, ref in enumerate((q_ref, k_ref, v_ref)):
        made = dims(own, weights_ref[n, own_rows, :], 1, 0) + dims(peer, weights_ref[n, other_rows, :], 1, 0)
        ref[...] = (made * factor if n == 0 else made).astype(bf16)

    def order(i):
        return jnp.where(i < late, i * 9 + 8, ((i - late) >> 3) * 9 + ((i - late) & 7))

    place = jnp.where(pads, 2 * total, order(iota((total, 1), 0)))
    column = iota((1, rows), 1) + late
    bias_ref[:, :rows] = jnp.where(place <= order(column), 0.0, MASKED)
    column = iota((1, 2 * late), 1) & (late - 1)
    bias_ref[:, rows:] = jnp.where(place <= order(column), 0.0, MASKED)
    left = iota((total, 2 * HDIM), 1) < HDIM
    block = rows // 2
    low = late + block

    def products(k, v, q, u, bias):
        return dims(k, q, 1, 1) + bias, dims(v, u, 1, 1)

    def softmax_grads(scores, grads):
        powers = jnp.exp(scores - jnp.max(scores, 0, keepdims=True))
        weights = powers * (1.0 / jnp.sum(powers, 0, keepdims=True))
        rounded = weights.astype(bf16)
        center = jnp.sum(rounded.astype(f32) * grads, 0, keepdims=True)
        return rounded, (weights * (grads - center)).astype(bf16)

    def pair(p, carry):
        start = p * 128 if isinstance(p, int) else pl.multiple_of(p * 128, 128)
        span = pl.ds(start, 128)
        q, k, v, u = q_ref[:, span], k_ref[:, span], v_ref[:, span], u_ref[:, span]
        blocks = []
        for side in (left, ~left):
            ks = jnp.where(side, k, 0).astype(bf16)
            vs = jnp.where(side, v, 0).astype(bf16)
            for reach, first in ((low, late), (total, low)):
                bias = (reach, slice(first - late, first - late + block))
                blocks.append((ks[:reach], vs[:reach], q[first : first + block], u[first : first + block], bias))
        side = left[:late]
        q_late = jnp.concatenate([jnp.where(side, q[:late], 0), jnp.where(side, 0, q[:late])], 0).astype(bf16)
        u_late = jnp.concatenate([jnp.where(side, u[:late], 0), jnp.where(side, 0, u[:late])], 0).astype(bf16)
        blocks.append((k, v, q_late, u_late, (total, slice(rows, rows + 2 * late))))
        found = []

        def begin(i):
            ks, vs, qs, us, (reach, columns) = blocks[i]
            return products(ks, vs, qs, us, bias_ref[:reach, columns])

        ready = begin(0)
        for i, (ks, _, qs, us, _) in enumerate(blocks):
            now = ready
            if i + 1 < len(blocks):
                ready = begin(i + 1)
            rounded, ds = softmax_grads(*now)
            found.append((dims(rounded, us, 1, 0), dims(ds, qs, 1, 0), dims(ks, ds, 0, 0)))
        ends = found.pop()
        (v00, k00, q00), (v01, k01, q01), (v10, k10, q10), (v11, k11, q11) = found
        for n, (a0, a1, b0, b1, end) in enumerate(((k00, k01, k10, k11, ends[1]), (v00, v01, v10, v11, ends[0]))):
            both = jnp.where(left, a1, b1) + end
            g_ref[n, :low, span] = (both[:low] + jnp.where(left[:low], a0, b0)).astype(bf16)
            g_ref[n, low:, span] = both[low:].astype(bf16)
        dq_ref[span, :block] = ((q00 + q10) * factor).astype(bf16)
        dq_ref[span, block:rows] = ((q01 + q11) * factor).astype(bf16)
        upper = iota((128, late), 0) < HDIM
        dq_ref[span, rows:] = (jnp.where(upper, ends[2][:, :late], ends[2][:, late:]) * factor).astype(bf16)
        return carry

    for p in range(half // 128):
        pair(p, 0)

    def partial_of(lines):
        rest = dims(g_ref[0], weights_ref[1, lines, :], 1, 1) + dims(g_ref[1], weights_ref[2, lines, :], 1, 1)
        main = dims(dq_ref[:, :rows], weights_ref[0, lines, :], 0, 1)
        ends = dims(dq_ref[:, rows:], weights_ref[0, lines, :], 0, 1)
        return (rest + jnp.concatenate([ends, main], 0)).astype(bf16)

    first = jnp.zeros((total, 1), f32)
    second = jnp.zeros((total, 1), f32)
    for lines, ref, normed in ((own_rows, keep_ref, own), (other_rows, send_ref, peer)):
        part = partial_of(lines)
        ref[:, :half] = part
        part = part.astype(f32)
        mine = (lines is own_rows) == (head == 0)
        gain = jnp.where(mine, gain_ref[:, :half], gain_ref[:, half:])
        first = first + jnp.sum(part * gain, -1, keepdims=True)
        second = second + jnp.sum(part * normed.astype(f32), -1, keepdims=True)
    lane = iota((total, 128), 1)
    stats_ref[...] = jnp.where(lane == 0, first, jnp.where(lane == 1, second, 0.0))
    split = jnp.zeros((total, 128), f32)
    for n, value in enumerate(thirds(first) + thirds(second)):
        split = jnp.where(lane == n, value, split)
    send_ref[:, half:] = split.astype(bf16)


def combine_kernel(head_ref, keep_ref, got_ref, own_ref, stats_ref, gain_ref, out_ref):
    total, half = keep_ref.shape
    rows = out_ref.shape[0]
    late = total - rows
    width = 2 * half
    head = head_ref[0]
    own = own_ref[...].astype(f32)
    gain = jnp.where(head == 0, gain_ref[:, :half], gain_ref[:, half:])
    split, stats = got_ref[:, half:].astype(f32), stats_ref[...]
    first = (stats[:, 0:1] + (split[:, 0:1] + split[:, 1:2] + split[:, 2:3])) / width
    second = (stats[:, 1:2] + (split[:, 3:4] + split[:, 4:5] + split[:, 5:6])) / width
    inverse = 1.0 / gain
    grad = keep_ref[...].astype(f32) + got_ref[:, :half].astype(f32)
    gain_sum = jnp.sum(grad * own, 0, keepdims=True) * inverse
    result = (grad * gain - first - own * inverse * second).astype(bf16)
    out_ref[:, :half] = result[late:]
    ext = jnp.zeros((rows, 128), f32)
    put_row, put_col = iota((rows, late), 0), iota((rows, late), 1)
    piece = iota((rows, 128), 0) & 7
    for i in range(4):
        span = slice(i * 128, (i + 1) * 128)
        put = (put_row == put_col * 8 + i).astype(bf16)
        ext = ext + dims(put, result[:late, span], 1, 0)
        ext = jnp.where(piece == i + 4, gain_sum[:, span], ext)
    out_ref[:, half:] = ext.astype(bf16)


def finish_kernel(slots, back_ref, labrow_ref, spread_ref, out_ref, gain_ref):
    tokens, half = out_ref.shape
    rows = back_ref.shape[0]
    labrow = labrow_ref[...]
    lab = column_of(labrow)
    before = (lab == labrow) & (iota((tokens, tokens), 1) < iota((tokens, tokens), 0))
    rank = jnp.sum(before.astype(f32), -1, keepdims=True).astype(jnp.int32)
    key = jnp.where(rank < slots - 1, lab * 8 + rank, -1)
    last = jnp.where(rank == slots - 1, lab, -1)
    col = iota((tokens, rows), 1)
    hot = (col == key).astype(bf16)
    hot_last = jnp.where((col >> 3) == last, col & 7, -1)
    spread = spread_ref[...]
    ext = back_ref[:, half:]
    piece = iota((rows, 128), 0) & 7
    for i in range(half // 128):
        span = slice(i * 128, (i + 1) * 128)
        value = dims(hot, back_ref[:, span], 1, 0)
        value = value + dims((hot_last == i).astype(bf16), ext, 1, 0)
        out_ref[:, span] = (value * spread).astype(bf16)
        gain_ref[:, span] = jnp.sum(jnp.where(piece == i + 4, ext.astype(f32), 0.0), 0, keepdims=True)


def attend_call(head, recv, peer, projection, gain):
    rows, half = recv.shape[0], projection.shape[2]
    total = rows + rows // 8
    shape = jax.ShapeDtypeStruct
    return vmem_call(
        attend_kernel,
        (
            shape((total, half), bf16),
            shape((total, half + 128), bf16),
            shape((total, half), bf16),
            shape((total, 128), f32),
        ),
        scratch=[
            pltpu.VMEM((total, half), bf16),
            pltpu.VMEM((total, half), bf16),
            pltpu.VMEM((total, half), bf16),
            pltpu.VMEM((total, half), bf16),
            pltpu.VMEM((total, half), bf16),
            pltpu.VMEM((2, total, half), bf16),
            pltpu.VMEM((half, total), bf16),
            pltpu.VMEM((total, rows + 2 * (total - rows)), f32),
        ],
        limit=26,
        scalars=1,
        count=4,
    )(head, recv, peer, projection, gain)


def on_device(hidden, norm_gain, projection, upstream, cluster):
    sources = lax.axis_size("seq")
    tokens, width = hidden.shape[1:]
    half = projection.shape[2]
    slots = 3 * tokens // sources
    total, rows = sources * slots, sources * 8
    head = lax.axis_index("head").astype(jnp.int32).reshape(1)
    gain = norm_gain.reshape(1, width)
    labrow = cluster.reshape(1, tokens)
    shape = jax.ShapeDtypeStruct
    swap = [(0, 1), (1, 0)]

    sent, spread = vmem_call(
        lambda *refs: pack_kernel(slots, *refs),
        (shape((rows, width + 128), bf16), shape((tokens, 1), f32)),
        scalars=1,
        count=4,
    )(head, hidden[0], gain, upstream[0], labrow)
    recv = lax.all_to_all(sent.reshape(sources, 8, width + 128), "seq", 0, 0, tiled=True)
    recv = recv.reshape(rows, width + 128)
    peer = lax.ppermute(recv, "head", swap)
    keep, send, own, stats = attend_call(head, recv, peer, projection, gain)
    got = lax.ppermute(send, "head", swap)
    answer = vmem_call(combine_kernel, shape((rows, half + 128), bf16), scalars=1, count=5)(
        head, keep, got, own, stats, gain
    )
    back = lax.all_to_all(answer.reshape(sources, 8, half + 128), "seq", 0, 0, tiled=True)
    back = back.reshape(rows, half + 128)
    result, gain_sum = vmem_call(
        lambda *refs: finish_kernel(slots, *refs),
        (shape((tokens, half), bf16), shape((1, half), f32)),
        count=3,
    )(back, labrow, spread)
    gain_gradient = lax.psum(gain_sum.reshape(half), "dp") * (sources * lax.axis_size("dp") * tokens) ** (-0.5)
    return (result.reshape(1, tokens, half), gain_gradient)


def solution(mesh):
    in_specs = (
        P("dp", "seq", None),
        P(),
        P(None, None, "head"),
        P("dp", "seq", "head"),
        P("dp", "seq", None),
    )
    out_specs = (P("dp", "seq", "head"), P("head"))
    return jax.shard_map(
        on_device, mesh=mesh, in_specs=in_specs, out_specs=out_specs, check_vma=False
    )
```

time: 187 us -> 166 us (0.89)
  the two profiles are of different devices: /device:TPU:32 before, /device:TPU:2 now
where the time goes in v2:
time: 166 us
  blocking collectives  134 us (81%)
  Pallas kernels  16.1 us (10%)
  local copies, waits for them, and re-layouts  5.18 us (3%)
  waiting for transfers between devices  4.47 us (3%)
  starting transfers between devices  4.35 us (3%)
    all_to_all x1, blocking collectives, on_device(): lax.all_to_all(sent.reshape(sources, 8, width + 128), 'seq', 0, 0, tiled=...  79.2 us
    all_to_all x1, blocking collectives, on_device(): lax.all_to_all(answer.reshape(sources, 8, half + 128), 'seq', 0, 0, tiled...  44.4 us
    pallas_call x1, Pallas kernels, attend_call(): vmem_call(attend_kernel, (shape((total, half), bf16), shape((total, half...  12.2 us
    psum x1, blocking collectives, on_device(): lax.psum(gain_sum.reshape(half), 'dp')  10.7 us
    unnamed x14, local copies, waits for them, and re-layouts  5.18 us
  transfers between devices with their start and end apart: 2, of which 2 were waited for; matrix products, arithmetic and copies ran while one was open for 0% of the time, Pallas kernels for 0%

profile of v2, /device:TPU:2, one launch (start us, length us, event | category | flops | bytes accessed | tf_op | source)
XLA Modules:
  0.0 165.7 jit_solution(4745806235831624719)
XLA Ops:
  0.6 0.0 copy-start.1
  0.6 1.0 copy-done.1
  1.6 0.0 copy-start.2
  1.6 0.9 copy-done.2
  2.6 0.0 copy-start.3
  2.6 0.7 copy-done.3
  3.2 0.0 copy-start.5
  3.2 0.7 copy-done.5
  3.9 1.4 shard_map.68
  5.3 0.0 copy-start.4
  5.3 79.2 %all_to_all.10 = bf16[64,8,1152]{2,1,0:T(8,128)(2,1)S(1)} all-to-all(bf16[64,8,1152]{2,1,0:T(8,128)(2,1)S(1)} %bitcast.15), channel_id=1, replica_groups=mesh['seq'=64,'head'=2,'dp'=4] {'seq'}, dimensions={0} | all-to-all | bytes 2359296 | tf_op jit(solution)/shard_map/all_to_all | solution.py:300
  84.5 2.1 %collective-permute-start = (bf16[512,1152]{1,0:T(8,128)(2,1)S(1)}, bf16[512,1152]{1,0:T(8,128)(2,1)S(1)}, u32[]{:S(2)}, u32[]{:S(2)}) collective-permute-start(bf16[512,1152]{1,0:T(8,128)(2,1)S(1)} %bitcast.11), channel_id=1, source_target_pairs={{0,4},{4,0},{1,5},{5,1},{2,6},{6,2},{3,7},{7,3},{8,12},{12,8},{9,1... | collective-permute-start | bytes 3538952 | tf_op jit(solution)/shard_map/ppermute | solution.py:302
  86.6 2.6 %collective-permute-done.other_ref = bf16[512,1152]{1,0:T(8,128)(2,1)S(1)} collective-permute-done((bf16[512,1152]{1,0:T(8,128)(2,1)S(1)}, bf16[512,1152]{1,0:T(8,128)(2,1)S(1)}, u32[]{:S(2)}, u32[]{:S(2)}) %collective-permute-start) | collective-permute-done | bytes 1179680 | tf_op jit(solution)/shard_map/ppermute | solution.py:302
  89.3 0.0 copy-done.4
  89.3 0.0 copy-start
  89.3 1.9 %copy-done = bf16[3,1024,512]{2,1,0:T(8,128)(2,1)S(1)} copy-done((bf16[3,1024,512]{2,1,0:T(8,128)(2,1)S(1)}, bf16[3,1024,512]{2,1,0:T(8,128)(2,1)}, u32[]{:S(2)}) %copy-start) | copy-done | bytes 3145752
  91.2 12.2 %shard_map.69 = (bf16[576,512]{1,0:T(8,128)(2,1)S(1)}, bf16[576,640]{1,0:T(8,128)(2,1)S(1)}, bf16[576,512]{1,0:T(8,128)(2,1)S(1)}, f32[576,128]{1,0:T(8,128)S(1)}) custom-call(s32[1]{0:T(128)} %bitcast.refs_0_.head_ref, bf16[512,1152]{1,0:T(8,128)(2,1)S(1)} %bitcast.12, bf16[512,1152]{1,0:T(8,128)(2,1)S(1)} %collective-permute-done.other_ref, ...), custom_call_target="tpu_custom_call" | custom-call | tf_op jit(solution)/shard_map/pallas_call | solution.py:258
  103.4 2.3 %collective-permute-start.1 = (bf16[576,640]{1,0:T(8,128)(2,1)S(1)}, bf16[576,640]{1,0:T(8,128)(2,1)S(1)}, u32[]{:S(2)}, u32[]{:S(2)}) collective-permute-start(bf16[576,640]{1,0:T(8,128)(2,1)S(1)} %get-tuple-element.12), channel_id=1, source_target_pairs={{0,4},{4,0},{1,5},{5,1},{2,6},{6,2},{3,7},{7,3},{8,12},{12,8},{9,1... | collective-permute-start | bytes 2211848 | tf_op jit(solution)/shard_map/ppermute | solution.py:304
  105.7 1.8 %collective-permute-done.1.got_ref = bf16[576,640]{1,0:T(8,128)(2,1)S(1)} collective-permute-done((bf16[576,640]{1,0:T(8,128)(2,1)S(1)}, bf16[576,640]{1,0:T(8,128)(2,1)S(1)}, u32[]{:S(2)}, u32[]{:S(2)}) %collective-permute-start.1) | collective-permute-done | bytes 737312 | tf_op jit(solution)/shard_map/ppermute | solution.py:304
  107.5 1.0 shard_map.70
  108.5 0.0 copy-start.6
  108.5 44.4 %all_to_all.11 = bf16[64,8,640]{2,1,0:T(8,128)(2,1)S(1)} all-to-all(bf16[64,8,640]{2,1,0:T(8,128)(2,1)S(1)} %bitcast.14), channel_id=1, replica_groups=mesh['seq'=64,'head'=2,'dp'=4] {'seq'}, dimensions={0} | all-to-all | bytes 1310720 | tf_op jit(solution)/shard_map/all_to_all | solution.py:308
  152.9 0.0 copy-done.6
  152.9 1.5 shard_map.71
  154.4 10.7 %psum.7 = f32[512]{0:T(512)S(1)} all-reduce(f32[512]{0:T(512)S(1)} %bitcast.23), channel_id=1, replica_groups=mesh['seq'=64,'head'=2,'dp'=4] {'dp'}, use_global_device_ids=true, to_apply=%region_0.0 | all-reduce | flops 512 | bytes 4096 | tf_op jit(solution)/shard_map/psum | solution.py:315
  165.1 0.6 broadcast_multiply_fusion
Async XLA Ops:
  0.6 1.0 copy-start.1
  1.6 0.9 copy-start.2
  2.6 0.7 copy-start.3
  3.2 0.7 copy-start.5
  5.3 84.0 %copy-start.4 = (f32[1024]{0:T(1024)S(1)}, f32[1024]{0:T(1024)}, u32[]{:S(2)}) copy-start(f32[1024]{0:T(1024)} %param.6) | copy-start | bytes 12292
  84.5 4.7 %collective-permute-start = (bf16[512,1152]{1,0:T(8,128)(2,1)S(1)}, bf16[512,1152]{1,0:T(8,128)(2,1)S(1)}, u32[]{:S(2)}, u32[]{:S(2)}) collective-permute-start(bf16[512,1152]{1,0:T(8,128)(2,1)S(1)} %bitcast.11), channel_id=1, source_target_pairs={{0,4},{4,0},{1,5},{5,1},{2,6},{6,2},{3,7},{7,3},{8,12},{12,8},{9,1... | collective-permute-start | bytes 3538952 | tf_op jit(solution)/shard_map/ppermute | solution.py:302
  89.3 1.9 %copy-start = (bf16[3,1024,512]{2,1,0:T(8,128)(2,1)S(1)}, bf16[3,1024,512]{2,1,0:T(8,128)(2,1)}, u32[]{:S(2)}) copy-start(bf16[3,1024,512]{2,1,0:T(8,128)(2,1)} %weights_ref.1) | copy-start | bytes 9437188
  103.4 4.1 %collective-permute-start.1 = (bf16[576,640]{1,0:T(8,128)(2,1)S(1)}, bf16[576,640]{1,0:T(8,128)(2,1)S(1)}, u32[]{:S(2)}, u32[]{:S(2)}) collective-permute-start(bf16[576,640]{1,0:T(8,128)(2,1)S(1)} %get-tuple-element.12), channel_id=1, source_target_pairs={{0,4},{4,0},{1,5},{5,1},{2,6},{6,2},{3,7},{7,3},{8,12},{12,8},{9,1... | collective-permute-start | bytes 2211848 | tf_op jit(solution)/shard_map/ppermute | solution.py:304
  108.5 44.4 %copy-start.6 = (s32[1,192,1]{1,2,0:T(1,128)S(1)}, s32[1,192,1]{1,2,0:T(1,128)}, u32[]{:S(2)}) copy-start(s32[1,192,1]{1,2,0:T(1,128)} %param.9) | copy-start | bytes 2308

commit v3 on v2

--- a/solution.py
+++ b/solution.py
@@ -21,12 +21,13 @@
     return lax.broadcasted_iota(jnp.int32, shape, dim)
 
 
-def vmem_call(kernel, out_shape, scratch=(), limit=8, scalars=0, count=1):
+def vmem_call(kernel, out_shape, scratch=(), limit=8, scalars=0, count=1, space=None):
     spec = pl.BlockSpec(memory_space=pltpu.VMEM)
+    source = spec if space is None else pl.BlockSpec(memory_space=space)
     return pl.pallas_call(
         kernel,
         out_shape=out_shape,
-        in_specs=[pl.BlockSpec(memory_space=pltpu.SMEM)] * scalars + [spec] * count,
+        in_specs=[pl.BlockSpec(memory_space=pltpu.SMEM)] * scalars + [source] * count,
         out_specs=jax.tree.map(lambda _: spec, out_shape),
         scratch_shapes=scratch,
         compiler_params=pltpu.CompilerParams(vmem_limit_bytes=limit * 2**20),
@@ -39,7 +40,24 @@
     return jnp.sum(jnp.where(same, labels.astype(f32), 0.0), -1, keepdims=True).astype(jnp.int32)
 
 
-def pack_kernel(slots, head_ref, hidden_ref, gain_ref, up_ref, labrow_ref, out_ref, spread_ref):
+def pack_kernel(slots, head_ref, hidden_any, gain_any, up_any, labrow_any, weights_any,
+                out_ref, spread_ref, gain_ref, labrow_ref, weights_ref, hidden_ref, up_ref, sems):
+    copies = [
+        pltpu.make_async_copy(source, target, sems.at[n])
+        for n, (source, target) in enumerate(
+            (
+                (labrow_any, labrow_ref),
+                (gain_any, gain_ref),
+                (hidden_any, hidden_ref),
+                (up_any, up_ref),
+                (weights_any, weights_ref),
+            )
+        )
+    ]
+    for copy in copies:
+        copy.start()
+    for copy in copies[:3]:
+        copy.wait()
     tokens, width = hidden_ref.shape
     half = width // 2
     x = hidden_ref[...].astype(f32)
@@ -48,6 +66,7 @@
     spread_ref[...] = spread
     normed = (center * spread * gain_ref[...]).astype(bf16)
     own = jnp.where(head_ref[0] == 0, normed[:, :half], normed[:, half:])
+    copies[3].wait()
     up = up_ref[...]
     labrow = labrow_ref[...]
     lab = column_of(labrow)
@@ -73,6 +92,7 @@
         total = total + dims(jnp.where(piece == i, hot_last, 0.0).astype(bf16), source, 1, 0)
     mark = (iota((rows, 128), 1) == 0) & ((iota((rows, 128), 0) & 7) == 4) & (taken == 0)
     out_ref[:, width:] = jnp.where(mark, PAD_MARK, total).astype(bf16)
+    copies[4].wait()
 
 
 def thirds(value):
@@ -228,7 +248,7 @@
     out_ref[:, half:] = ext.astype(bf16)
 
 
-def finish_kernel(slots, back_ref, labrow_ref, spread_ref, out_ref, gain_ref):
+def finish_kernel(slots, scale, back_ref, labrow_ref, spread_ref, out_ref, gain_ref):
     tokens, half = out_ref.shape
     rows = back_ref.shape[0]
     labrow = labrow_ref[...]
@@ -248,7 +268,7 @@
         value = dims(hot, back_ref[:, span], 1, 0)
         value = value + dims((hot_last == i).astype(bf16), ext, 1, 0)
         out_ref[:, span] = (value * spread).astype(bf16)
-        gain_ref[:, span] = jnp.sum(jnp.where(piece == i + 4, ext.astype(f32), 0.0), 0, keepdims=True)
+        gain_ref[:, span] = scale * jnp.sum(jnp.where(piece == i + 4, ext.astype(f32), 0.0), 0, keepdims=True)
 
 
 def attend_call(head, recv, peer, projection, gain):
@@ -286,21 +306,33 @@
     slots = 3 * tokens // sources
     total, rows = sources * slots, sources * 8
     head = lax.axis_index("head").astype(jnp.int32).reshape(1)
-    gain = norm_gain.reshape(1, width)
-    labrow = cluster.reshape(1, tokens)
     shape = jax.ShapeDtypeStruct
     swap = [(0, 1), (1, 0)]
-
-    sent, spread = vmem_call(
+    scale = (sources * lax.axis_size("dp") * tokens) ** (-0.5)
+
+    sent, spread, gain, labrow, weights = vmem_call(
         lambda *refs: pack_kernel(slots, *refs),
-        (shape((rows, width + 128), bf16), shape((tokens, 1), f32)),
+        (
+            shape((rows, width + 128), bf16),
+            shape((tokens, 1), f32),
+            shape((1, width), f32),
+            shape((1, tokens), jnp.int32),
+            shape(projection.shape, bf16),
+        ),
+        scratch=[
+            pltpu.VMEM((tokens, width), bf16),
+            pltpu.VMEM((tokens, half), bf16),
+            pltpu.SemaphoreType.DMA((5,)),
+        ],
+        limit=12,
         scalars=1,
-        count=4,
-    )(head, hidden[0], gain, upstream[0], labrow)
+        count=5,
+        space=pltpu.HBM,
+    )(head, *[pltpu.with_memory_space_constraint(v, pltpu.HBM) for v in (hidden[0], norm_gain.reshape(1, width), upstream[0], cluster.reshape(1, tokens), projection)])
     recv = lax.all_to_all(sent.reshape(sources, 8, width + 128), "seq", 0, 0, tiled=True)
     recv = recv.reshape(rows, width + 128)
     peer = lax.ppermute(recv, "head", swap)
-    keep, send, own, stats = attend_call(head, recv, peer, projection, gain)
+    keep, send, own, stats = attend_call(head, recv, peer, weights, gain)
     got = lax.ppermute(send, "head", swap)
     answer = vmem_call(combine_kernel, shape((rows, half + 128), bf16), scalars=1, count=5)(
         head, keep, got, own, stats, gain
@@ -308,11 +340,11 @@
     back = lax.all_to_all(answer.reshape(sources, 8, half + 128), "seq", 0, 0, tiled=True)
     back = back.reshape(rows, half + 128)
     result, gain_sum = vmem_call(
-        lambda *refs: finish_kernel(slots, *refs),
+        lambda *refs: finish_kernel(slots, scale, *refs),
         (shape((tokens, half), bf16), shape((1, half), f32)),
         count=3,
     )(back, labrow, spread)
-    gain_gradient = lax.psum(gain_sum.reshape(half), "dp") * (sources * lax.axis_size("dp") * tokens) ** (-0.5)
+    gain_gradient = lax.psum(gain_sum.reshape(half), "dp")
     return (result.reshape(1, tokens, half), gain_gradient)
 
 

time: 166 us -> 162 us (0.976)
  local copies, waits for them, and re-layouts: 5.18 us -> 0 us
    unnamed x14 -> x0, local copies, waits for them, and re-layouts: 5.18 us -> none
where the time goes in v3:
time: 162 us
  blocking collectives  135 us (83%)
  Pallas kernels  17.2 us (11%)
  waiting for transfers between devices  4.47 us (3%)
  starting transfers between devices  4.35 us (3%)
    all_to_all x1, blocking collectives, on_device(): lax.all_to_all(sent.reshape(sources, 8, width + 128), 'seq', 0, 0, tiled=...  79.2 us
    all_to_all x1, blocking collectives, on_device(): lax.all_to_all(answer.reshape(sources, 8, half + 128), 'seq', 0, 0, tiled...  44.4 us
    pallas_call x1, Pallas kernels, attend_call(): vmem_call(attend_kernel, (shape((total, half), bf16), shape((total, half...  12.2 us
    psum x1, blocking collectives, on_device(): gain_gradient = lax.psum(gain_sum.reshape(half), 'dp')  11.3 us
  transfers between devices with their start and end apart: 2, of which 2 were waited for; matrix products, arithmetic and copies ran while one was open for 0% of the time, Pallas kernels for 0%

profile of v3, /device:TPU:2, one launch (start us, length us, event | category | flops | bytes accessed | tf_op | source)
XLA Modules:
  0.0 161.6 jit_solution(14482894443656697873)
XLA Ops:
  0.6 2.5 %shard_map.68 = (bf16[512,1152]{1,0:T(8,128)(2,1)S(1)}, f32[192,1]{1,0:T(8,128)S(1)}, f32[1,1024]{1,0:T(1,128)S(1)}, s32[1,192]{1,0:T(1,128)S(1)}, bf16[3,1024,512]{2,1,0:T(8,128)(2,1)S(1)}) custom-call(s32[1]{0:T(128)} %bitcast.refs_0_.head_ref, bf16[192,1024]{1,0:T(8,128)(2,1)} %bitcast.17, f32[1,1024]{1,0:T(1,128)} %bitcast.19, ...), custom_call_target="tpu_custom_call" | custom-call | tf_op jit(solution)/shard_map/pallas_call | solution.py:313
  3.1 79.2 %all_to_all.10 = bf16[64,8,1152]{2,1,0:T(8,128)(2,1)S(1)} all-to-all(bf16[64,8,1152]{2,1,0:T(8,128)(2,1)S(1)} %bitcast.15), channel_id=1, replica_groups=mesh['seq'=64,'head'=2,'dp'=4] {'seq'}, dimensions={0} | all-to-all | bytes 2359296 | tf_op jit(solution)/shard_map/all_to_all | solution.py:332
  82.4 2.1 %collective-permute-start = (bf16[512,1152]{1,0:T(8,128)(2,1)S(1)}, bf16[512,1152]{1,0:T(8,128)(2,1)S(1)}, u32[]{:S(2)}, u32[]{:S(2)}) collective-permute-start(bf16[512,1152]{1,0:T(8,128)(2,1)S(1)} %bitcast.11), channel_id=1, source_target_pairs={{0,4},{4,0},{1,5},{5,1},{2,6},{6,2},{3,7},{7,3},{8,12},{12,8},{9,1... | collective-permute-start | bytes 3538952 | tf_op jit(solution)/shard_map/ppermute | solution.py:334
  84.5 2.6 %collective-permute-done.other_ref = bf16[512,1152]{1,0:T(8,128)(2,1)S(1)} collective-permute-done((bf16[512,1152]{1,0:T(8,128)(2,1)S(1)}, bf16[512,1152]{1,0:T(8,128)(2,1)S(1)}, u32[]{:S(2)}, u32[]{:S(2)}) %collective-permute-start) | collective-permute-done | bytes 1179680 | tf_op jit(solution)/shard_map/ppermute | solution.py:334
  87.1 12.2 %shard_map.69 = (bf16[576,512]{1,0:T(8,128)(2,1)S(1)}, bf16[576,640]{1,0:T(8,128)(2,1)S(1)}, bf16[576,512]{1,0:T(8,128)(2,1)S(1)}, f32[576,128]{1,0:T(8,128)S(1)}) custom-call(s32[1]{0:T(128)} %bitcast.refs_0_.head_ref, bf16[512,1152]{1,0:T(8,128)(2,1)S(1)} %bitcast.12, bf16[512,1152]{1,0:T(8,128)(2,1)S(1)} %collective-permute-done.other_ref, ...), custom_call_target="tpu_custom_call" | custom-call | tf_op jit(solution)/shard_map/pallas_call | solution.py:278
  99.4 2.3 %collective-permute-start.1 = (bf16[576,640]{1,0:T(8,128)(2,1)S(1)}, bf16[576,640]{1,0:T(8,128)(2,1)S(1)}, u32[]{:S(2)}, u32[]{:S(2)}) collective-permute-start(bf16[576,640]{1,0:T(8,128)(2,1)S(1)} %get-tuple-element.17), channel_id=1, source_target_pairs={{0,4},{4,0},{1,5},{5,1},{2,6},{6,2},{3,7},{7,3},{8,12},{12,8},{9,1... | collective-permute-start | bytes 2211848 | tf_op jit(solution)/shard_map/ppermute | solution.py:336
  101.6 1.8 %collective-permute-done.1.got_ref = bf16[576,640]{1,0:T(8,128)(2,1)S(1)} collective-permute-done((bf16[576,640]{1,0:T(8,128)(2,1)S(1)}, bf16[576,640]{1,0:T(8,128)(2,1)S(1)}, u32[]{:S(2)}, u32[]{:S(2)}) %collective-permute-start.1) | collective-permute-done | bytes 737312 | tf_op jit(solution)/shard_map/ppermute | solution.py:336
  103.5 1.0 shard_map.70
  104.5 44.4 %all_to_all.11 = bf16[64,8,640]{2,1,0:T(8,128)(2,1)S(1)} all-to-all(bf16[64,8,640]{2,1,0:T(8,128)(2,1)S(1)} %bitcast.14), channel_id=1, replica_groups=mesh['seq'=64,'head'=2,'dp'=4] {'seq'}, dimensions={0} | all-to-all | bytes 1310720 | tf_op jit(solution)/shard_map/all_to_all | solution.py:340
  148.8 1.5 shard_map.71
  150.3 11.3 %psum.7 = f32[512]{0:T(512)} all-reduce(f32[512]{0:T(512)S(1)} %bitcast.16), channel_id=1, replica_groups=mesh['seq'=64,'head'=2,'dp'=4] {'dp'}, use_global_device_ids=true, to_apply=%region_0.0 | all-reduce | flops 512 | bytes 4096 | tf_op jit(solution)/shard_map/psum | solution.py:347
Async XLA Ops:
  82.4 4.7 %collective-permute-start = (bf16[512,1152]{1,0:T(8,128)(2,1)S(1)}, bf16[512,1152]{1,0:T(8,128)(2,1)S(1)}, u32[]{:S(2)}, u32[]{:S(2)}) collective-permute-start(bf16[512,1152]{1,0:T(8,128)(2,1)S(1)} %bitcast.11), channel_id=1, source_target_pairs={{0,4},{4,0},{1,5},{5,1},{2,6},{6,2},{3,7},{7,3},{8,12},{12,8},{9,1... | collective-permute-start | bytes 3538952 | tf_op jit(solution)/shard_map/ppermute | solution.py:334
  99.4 4.1 %collective-permute-start.1 = (bf16[576,640]{1,0:T(8,128)(2,1)S(1)}, bf16[576,640]{1,0:T(8,128)(2,1)S(1)}, u32[]{:S(2)}, u32[]{:S(2)}) collective-permute-start(bf16[576,640]{1,0:T(8,128)(2,1)S(1)} %get-tuple-element.17), channel_id=1, source_target_pairs={{0,4},{4,0},{1,5},{5,1},{2,6},{6,2},{3,7},{7,3},{8,12},{12,8},{9,1... | collective-permute-start | bytes 2211848 | tf_op jit(solution)/shard_map/ppermute | solution.py:336

commit v4 on v3

--- a/solution.py
+++ b/solution.py
@@ -21,16 +21,17 @@
     return lax.broadcasted_iota(jnp.int32, shape, dim)
 
 
-def vmem_call(kernel, out_shape, scratch=(), limit=8, scalars=0, count=1, space=None):
+def vmem_call(kernel, out_shape, scratch=(), limit=8, scalars=0, count=1, space=pltpu.VMEM, cost=None):
     spec = pl.BlockSpec(memory_space=pltpu.VMEM)
-    source = spec if space is None else pl.BlockSpec(memory_space=space)
+    spaces = space if isinstance(space, tuple) else (space,) * count
     return pl.pallas_call(
         kernel,
         out_shape=out_shape,
-        in_specs=[pl.BlockSpec(memory_space=pltpu.SMEM)] * scalars + [source] * count,
+        in_specs=[pl.BlockSpec(memory_space=pltpu.SMEM)] * scalars + [pl.BlockSpec(memory_space=m) for m in spaces],
         out_specs=jax.tree.map(lambda _: spec, out_shape),
         scratch_shapes=scratch,
         compiler_params=pltpu.CompilerParams(vmem_limit_bytes=limit * 2**20),
+        cost_estimate=cost and pl.CostEstimate(flops=0, bytes_accessed=cost, transcendentals=0),
     )
 
 
@@ -40,59 +41,59 @@
     return jnp.sum(jnp.where(same, labels.astype(f32), 0.0), -1, keepdims=True).astype(jnp.int32)
 
 
-def pack_kernel(slots, head_ref, hidden_any, gain_any, up_any, labrow_any, weights_any,
-                out_ref, spread_ref, gain_ref, labrow_ref, weights_ref, hidden_ref, up_ref, sems):
+def pack_kernel(slots, head_ref, hidden_any, gain_any, up_any, labrow_any,
+                out_ref, spread_ref, gain_ref, labrow_ref, hidden_ref, up_ref, sems):
     copies = [
         pltpu.make_async_copy(source, target, sems.at[n])
         for n, (source, target) in enumerate(
             (
                 (labrow_any, labrow_ref),
+                (up_any, up_ref),
+                (hidden_any, hidden_ref),
                 (gain_any, gain_ref),
-                (hidden_any, hidden_ref),
-                (up_any, up_ref),
-                (weights_any, weights_ref),
             )
         )
     ]
     for copy in copies:
         copy.start()
-    for copy in copies[:3]:
-        copy.wait()
+    copies[0].wait()
     tokens, width = hidden_ref.shape
     half = width // 2
+    rows = out_ref.shape[0]
+    labrow = labrow_ref[...]
+    lab = column_of(labrow)
+    before = (lab == labrow) & (iota((tokens, tokens), 0) < iota((tokens, tokens), 1))
+    rank = jnp.sum(before.astype(f32), 0, keepdims=True).astype(jnp.int32)
+    key = jnp.where(rank < slots - 1, labrow * 8 + rank, -1)
+    last = jnp.where(rank == slots - 1, labrow, -1)
+    row = iota((rows, tokens), 0)
+    hot = (row == key).astype(f32)
+    empty = jnp.sum(hot, -1, keepdims=True) == 0
+    hot = hot.astype(bf16)
+    hot_last = (row >> 3) == last
+    empty_last = jnp.sum(hot_last.astype(f32), -1, keepdims=True) == 0
+    pieces = [(hot_last & ((row & 7) == i)).astype(bf16) for i in range(8)]
+    copies[1].wait()
+    up = up_ref[...]
+    right = dims(hot, up, 1, 0)
+    first = iota((rows, half), 1) == 0
+    out_ref[:, half:width] = jnp.where(first & empty, PAD_MARK, right).astype(bf16)
+    total = jnp.zeros((rows, 128), f32)
+    for i in range(4):
+        total = total + dims(pieces[i + 4], up[:, i * 128 : (i + 1) * 128], 1, 0)
+    copies[2].wait()
+    copies[3].wait()
     x = hidden_ref[...].astype(f32)
     center = x - jnp.mean(x, -1, keepdims=True)
     spread = lax.rsqrt(jnp.mean(center * center, -1, keepdims=True) + EPSILON)
     spread_ref[...] = spread
     normed = (center * spread * gain_ref[...]).astype(bf16)
     own = jnp.where(head_ref[0] == 0, normed[:, :half], normed[:, half:])
-    copies[3].wait()
-    up = up_ref[...]
-    labrow = labrow_ref[...]
-    lab = column_of(labrow)
-    before = (lab == labrow) & (iota((tokens, tokens), 0) < iota((tokens, tokens), 1))
-    rank = jnp.sum(before.astype(f32), 0, keepdims=True).astype(jnp.int32)
-    rows = out_ref.shape[0]
-    key = jnp.where(rank < slots - 1, labrow * 8 + rank, -1)
-    last = jnp.where(rank == slots - 1, labrow, -1)
-    row = iota((rows, tokens), 0)
-    hot = (row == key).astype(f32)
-    taken = jnp.sum(hot, -1, keepdims=True)
-    hot = hot.astype(bf16)
     out_ref[:, :half] = dims(hot, own, 1, 0).astype(bf16)
-    right = dims(hot, up, 1, 0)
-    first = iota((rows, half), 1) == 0
-    out_ref[:, half:width] = jnp.where(first & (taken == 0), PAD_MARK, right).astype(bf16)
-    hot_last = ((row >> 3) == last).astype(f32)
-    taken = jnp.sum(hot_last, -1, keepdims=True)
-    piece = iota((rows, tokens), 0) & 7
-    total = jnp.zeros((rows, 128), f32)
-    for i in range(8):
-        source = (own if i < 4 else up)[:, (i % 4) * 128 : (i % 4 + 1) * 128]
-        total = total + dims(jnp.where(piece == i, hot_last, 0.0).astype(bf16), source, 1, 0)
-    mark = (iota((rows, 128), 1) == 0) & ((iota((rows, 128), 0) & 7) == 4) & (taken == 0)
+    for i in range(4):
+        total = total + dims(pieces[i], own[:, i * 128 : (i + 1) * 128], 1, 0)
+    mark = (iota((rows, 128), 1) == 0) & ((iota((rows, 128), 0) & 7) == 4) & empty_last
     out_ref[:, width:] = jnp.where(mark, PAD_MARK, total).astype(bf16)
-    copies[4].wait()
 
 
 def thirds(value):
@@ -102,44 +103,60 @@
     return high.astype(f32), middle.astype(f32), rest - middle.astype(f32)
 
 
-def attend_kernel(head_ref, recv_ref, other_ref, weights_ref, gain_ref, keep_ref, send_ref, own_ref, stats_ref,
-                  peer_ref, u_ref, q_ref, k_ref, v_ref, g_ref, dq_ref, bias_ref):
-    rows, extended = recv_ref.shape
+def own_kernel(head_ref, recv_ref, weights_ref, own_ref, u_ref, bias_ref, acc_ref):
+    rows = recv_ref.shape[0]
+    half = weights_ref.shape[2]
+    width = 2 * half
+    late = rows // 8
+    total = rows + late
+    pick_col, pick_row = iota((late, rows), 1), iota((late, rows), 0)
+    own_ref[late:, :] = recv_ref[:, :half]
+    u_ref[late:, :] = recv_ref[:, half:width]
+    for i in range(4):
+        span = slice(i * 128, (i + 1) * 128)
+        pick = (pick_col == pick_row * 8 + i).astype(bf16)
+        own_ref[:late, span] = dims(pick, recv_ref[:, width:], 1, 0).astype(bf16)
+        pick = (pick_col == pick_row * 8 + (i + 4)).astype(bf16)
+        u_ref[:late, span] = dims(pick, recv_ref[:, width:], 1, 0).astype(bf16)
+    up = u_ref[:, :128].astype(f32)
+    pads = up[:, :1] > 0.5 * PAD_MARK
+    u_ref[:, :128] = jnp.where(pads & (iota((total, 128), 1) == 0), 0.0, up).astype(bf16)
+    own_rows = pl.ds(pl.multiple_of(head_ref[0] * half, half), half)
+    own = own_ref[...]
+    for n in range(3):
+        acc_ref[n] = dims(own, weights_ref[n, own_rows, :], 1, 0)
+
+    def order(i):
+        return jnp.where(i < late, i * 9 + 8, ((i - late) >> 3) * 9 + ((i - late) & 7))
+
+    place = jnp.where(pads, 2 * total, order(iota((total, 1), 0)))
+    column = iota((1, rows), 1) + late
+    bias_ref[:, :rows] = jnp.where(place <= order(column), 0.0, MASKED)
+    column = iota((1, 2 * late), 1) & (late - 1)
+    bias_ref[:, rows:] = jnp.where(place <= order(column), 0.0, MASKED)
+
+
+def attend_kernel(head_ref, other_ref, own_ref, u_ref, bias_ref, acc_ref, weights_ref, gain_ref,
+                  keep_ref, send_ref, stats_ref, peer_ref, q_ref, k_ref, v_ref, g_ref, dq_ref):
+    rows = other_ref.shape[0]
     half = weights_ref.shape[2]
     width = 2 * half
     late = rows // 8
     total = rows + late
     head = head_ref[0]
     pick_col, pick_row = iota((late, rows), 1), iota((late, rows), 0)
-    own_ref[late:, :] = recv_ref[:, :half]
     peer_ref[late:, :] = other_ref[:, :half]
-    u_ref[late:, :] = recv_ref[:, half:width]
-    for i in range(4):
-        span = slice(i * 128, (i + 1) * 128)
+    for i in range(4):
         pick = (pick_col == pick_row * 8 + i).astype(bf16)
-        own_ref[:late, span] = dims(pick, recv_ref[:, width:], 1, 0).astype(bf16)
-        peer_ref[:late, span] = dims(pick, other_ref[:, width:], 1, 0).astype(bf16)
-        pick = (pick_col == pick_row * 8 + (i + 4)).astype(bf16)
-        u_ref[:late, span] = dims(pick, recv_ref[:, width:], 1, 0).astype(bf16)
-    up = u_ref[:, :128].astype(f32)
-    pads = up[:, :1] > 0.5 * PAD_MARK
-    u_ref[:, :128] = jnp.where(pads & (iota((total, 128), 1) == 0), 0.0, up).astype(bf16)
+        peer_ref[:late, i * 128 : (i + 1) * 128] = dims(pick, other_ref[:, width:], 1, 0).astype(bf16)
     own_rows = pl.ds(pl.multiple_of(head * half, half), half)
     other_rows = pl.ds(pl.multiple_of((1 - head) * half, half), half)
     own, peer = own_ref[...], peer_ref[...]
     factor = HDIM**-0.5
     for n, ref in enumerate((q_ref, k_ref, v_ref)):
-        made = dims(own, weights_ref[n, own_rows, :], 1, 0) + dims(peer, weights_ref[n, other_rows, :], 1, 0)
+        made = acc_ref[n] + dims(peer, weights_ref[n, other_rows, :], 1, 0)
         ref[...] = (made * factor if n == 0 else made).astype(bf16)
 
-    def order(i):
-        return jnp.where(i < late, i * 9 + 8, ((i - late) >> 3) * 9 + ((i - late) & 7))
-
-    place = jnp.where(pads, 2 * total, order(iota((total, 1), 0)))
-    column = iota((1, rows), 1) + late
-    bias_ref[:, :rows] = jnp.where(place <= order(column), 0.0, MASKED)
-    column = iota((1, 2 * late), 1) & (late - 1)
-    bias_ref[:, rows:] = jnp.where(place <= order(column), 0.0, MASKED)
     left = iota((total, 2 * HDIM), 1) < HDIM
     block = rows // 2
     low = late + block
@@ -248,9 +265,10 @@
     out_ref[:, half:] = ext.astype(bf16)
 
 
-def finish_kernel(slots, scale, back_ref, labrow_ref, spread_ref, out_ref, gain_ref):
-    tokens, half = out_ref.shape
-    rows = back_ref.shape[0]
+def prepare_kernel(slots, weights_any, labrow_ref, weights_ref, hot_ref, sem):
+    copy = pltpu.make_async_copy(weights_any, weights_ref, sem)
+    copy.start()
+    tokens, rows = hot_ref.shape[1:]
     labrow = labrow_ref[...]
     lab = column_of(labrow)
     before = (lab == labrow) & (iota((tokens, tokens), 1) < iota((tokens, tokens), 0))
@@ -258,45 +276,68 @@
     key = jnp.where(rank < slots - 1, lab * 8 + rank, -1)
     last = jnp.where(rank == slots - 1, lab, -1)
     col = iota((tokens, rows), 1)
-    hot = (col == key).astype(bf16)
     hot_last = jnp.where((col >> 3) == last, col & 7, -1)
+    hot_ref[4] = (col == key).astype(bf16)
+    for i in range(4):
+        hot_ref[i] = (hot_last == i).astype(bf16)
+    copy.wait()
+
+
+def finish_kernel(scale, back_ref, hot_ref, spread_ref, out_ref, gain_ref):
+    half = out_ref.shape[1]
+    rows = back_ref.shape[0]
     spread = spread_ref[...]
     ext = back_ref[:, half:]
     piece = iota((rows, 128), 0) & 7
     for i in range(half // 128):
         span = slice(i * 128, (i + 1) * 128)
-        value = dims(hot, back_ref[:, span], 1, 0)
-        value = value + dims((hot_last == i).astype(bf16), ext, 1, 0)
+        value = dims(hot_ref[4], back_ref[:, span], 1, 0) + dims(hot_ref[i], ext, 1, 0)
         out_ref[:, span] = (value * spread).astype(bf16)
         gain_ref[:, span] = scale * jnp.sum(jnp.where(piece == i + 4, ext.astype(f32), 0.0), 0, keepdims=True)
 
 
-def attend_call(head, recv, peer, projection, gain):
+def own_call(head, recv, projection):
     rows, half = recv.shape[0], projection.shape[2]
     total = rows + rows // 8
     shape = jax.ShapeDtypeStruct
     return vmem_call(
-        attend_kernel,
+        own_kernel,
         (
             shape((total, half), bf16),
-            shape((total, half + 128), bf16),
             shape((total, half), bf16),
-            shape((total, 128), f32),
+            shape((total, rows + 2 * (total - rows)), f32),
+            shape((3, total, half), f32),
         ),
+        limit=20,
+        cost=6 * 10**6,
+        scalars=1,
+        count=2,
+    )(head, recv, projection)
+
+
+def attend_call(head, peer, own, up, bias, acc, projection, gain):
+    rows, half = peer.shape[0], projection.shape[2]
+    total = rows + rows // 8
+    shape = jax.ShapeDtypeStruct
+    return vmem_call(
+        attend_kernel,
+        (shape((total, half), bf16), shape((total, half + 128), bf16), shape((total, 128), f32)),
         scratch=[
-            pltpu.VMEM((total, half), bf16),
             pltpu.VMEM((total, half), bf16),
             pltpu.VMEM((total, half), bf16),
             pltpu.VMEM((total, half), bf16),
             pltpu.VMEM((total, half), bf16),
             pltpu.VMEM((2, total, half), bf16),
             pltpu.VMEM((half, total), bf16),
-            pltpu.VMEM((total, rows + 2 * (total - rows)), f32),
         ],
         limit=26,
         scalars=1,
-        count=4,
-    )(head, recv, peer, projection, gain)
+        count=7,
+    )(head, peer, own, up, bias, acc, projection, gain)
+
+
+def in_hbm(array):
+    return pltpu.with_memory_space_constraint(array, pltpu.HBM)
 
 
 def on_device(hidden, norm_gain, projection, upstream, cluster):
@@ -310,29 +351,37 @@
     swap = [(0, 1), (1, 0)]
     scale = (sources * lax.axis_size("dp") * tokens) ** (-0.5)
 
-    sent, spread, gain, labrow, weights = vmem_call(
+    sent, spread, gain, labrow = vmem_call(
         lambda *refs: pack_kernel(slots, *refs),
         (
             shape((rows, width + 128), bf16),
             shape((tokens, 1), f32),
             shape((1, width), f32),
             shape((1, tokens), jnp.int32),
-            shape(projection.shape, bf16),
         ),
         scratch=[
             pltpu.VMEM((tokens, width), bf16),
             pltpu.VMEM((tokens, half), bf16),
-            pltpu.SemaphoreType.DMA((5,)),
+            pltpu.SemaphoreType.DMA((4,)),
         ],
-        limit=12,
         scalars=1,
-        count=5,
+        count=4,
         space=pltpu.HBM,
-    )(head, *[pltpu.with_memory_space_constraint(v, pltpu.HBM) for v in (hidden[0], norm_gain.reshape(1, width), upstream[0], cluster.reshape(1, tokens), projection)])
+    )(head, *[in_hbm(v) for v in (hidden[0], norm_gain.reshape(1, width), upstream[0], cluster.reshape(1, tokens))])
+    weights, hots = vmem_call(
+        lambda *refs: prepare_kernel(slots, *refs),
+        (shape(projection.shape, bf16), shape((5, tokens, rows), bf16)),
+        scratch=[pltpu.SemaphoreType.DMA(())],
+        cost=6 * 10**6,
+        scalars=0,
+        count=2,
+        space=(pltpu.HBM, pltpu.VMEM),
+    )(in_hbm(projection), labrow)
     recv = lax.all_to_all(sent.reshape(sources, 8, width + 128), "seq", 0, 0, tiled=True)
-    recv = recv.reshape(rows, width + 128)
+    recv, weights, hots = lax.optimization_barrier((recv.reshape(rows, width + 128), weights, hots))
     peer = lax.ppermute(recv, "head", swap)
-    keep, send, own, stats = attend_call(head, recv, peer, weights, gain)
+    own, up, bias, acc = own_call(head, recv, weights)
+    keep, send, stats = attend_call(head, peer, own, up, bias, acc, weights, gain)
     got = lax.ppermute(send, "head", swap)
     answer = vmem_call(combine_kernel, shape((rows, half + 128), bf16), scalars=1, count=5)(
         head, keep, got, own, stats, gain
@@ -340,10 +389,10 @@
     back = lax.all_to_all(answer.reshape(sources, 8, half + 128), "seq", 0, 0, tiled=True)
     back = back.reshape(rows, half + 128)
     result, gain_sum = vmem_call(
-        lambda *refs: finish_kernel(slots, scale, *refs),
+        lambda *refs: finish_kernel(scale, *refs),
         (shape((tokens, half), bf16), shape((1, half), f32)),
         count=3,
-    )(back, labrow, spread)
+    )(back, hots, spread)
     gain_gradient = lax.psum(gain_sum.reshape(half), "dp")
     return (result.reshape(1, tokens, half), gain_gradient)
 

time: 162 us -> 163 us (level)
  blocking collectives: 135 us -> 55.9 us
  waiting for transfers between devices: 4.47 us -> 59.6 us
  starting transfers between devices: 4.35 us -> 23.4 us
  Pallas kernels: 17.2 us -> 22.3 us
    all_to_all x1 -> x0, blocking collectives: 79.2 us -> none  [on_device(): lax.all_to_all(sent.reshape(sources, 8, width + 128), 'seq', 0, 0, tiled=...]
    all_to_all x0 -> x1, waiting for transfers between devices: none -> 57.9 us  [on_device(): lax.all_to_all(sent.reshape(sources, 8, width + 128), 'seq', 0, 0, tiled=...]
    all_to_all x0 -> x1, starting transfers between devices: none -> 18.8 us  [on_device(): lax.all_to_all(sent.reshape(sources, 8, width + 128), 'seq', 0, 0, tiled=...]
    pallas_call x1 -> x3, Pallas kernels: 1.48 us -> 5.91 us  [the longest x1 2.69 us: own_call(): vmem_call(own_kernel, (shape((total, half), bf16), shape((total, half), b...]
    ppermute x1, waiting for transfers between devices: 2.63 us -> 0.15 us  [on_device(): peer = lax.ppermute(recv, 'head', swap)]
  transfers between devices with their start and end apart: 2 -> 3, of which waited for: 2 -> 3; matrix products, arithmetic and copies ran while one was open for 0% -> 0% of each run, Pallas kernels for 0% -> 3%
where the time goes in v4:
time: 163 us
  waiting for transfers between devices  59.6 us (37%)
  blocking collectives  55.9 us (34%)
  starting transfers between devices  23.4 us (14%)
  Pallas kernels  22.3 us (14%)
    all_to_all x1, waiting for transfers between devices, on_device(): lax.all_to_all(sent.reshape(sources, 8, width + 128), 'seq', 0, 0, tiled=...  57.9 us
    all_to_all x1, blocking collectives, on_device(): lax.all_to_all(answer.reshape(sources, 8, half + 128), 'seq', 0, 0, tiled...  44.6 us
    all_to_all x1, starting transfers between devices, on_device(): lax.all_to_all(sent.reshape(sources, 8, width + 128), 'seq', 0, 0, tiled=...  18.8 us
    pallas_call x1, Pallas kernels, attend_call(): vmem_call(attend_kernel, (shape((total, half), bf16), shape((total, half...  11.5 us
    psum x1, blocking collectives, on_device(): gain_gradient = lax.psum(gain_sum.reshape(half), 'dp')  11.3 us
    pallas_call x1, Pallas kernels, on_device(): vmem_call(lambda *refs: pack_kernel(slots, *refs), (shape((rows, width +...  3.96 us
  transfers between devices with their start and end apart: 3, of which 3 were waited for; matrix products, arithmetic and copies ran while one was open for 0% of the time, Pallas kernels for 3%

profile of v4, /device:TPU:2, one launch (start us, length us, event | category | flops | bytes accessed | tf_op | source)
XLA Modules:
  0.0 162.9 jit_solution(8512843649493543141)
XLA Ops:
  0.6 4.0 %shard_map.68 = (bf16[512,1152]{1,0:T(8,128)(2,1)}, f32[192,1]{1,0:T(8,128)S(1)}, f32[1,1024]{1,0:T(1,128)S(1)}, s32[1,192]{1,0:T(1,128)S(1)}) custom-call(s32[1]{0:T(128)} %bitcast.refs_0_.head_ref, bf16[192,1024]{1,0:T(8,128)(2,1)} %bitcast.14, f32[1,1024]{1,0:T(1,128)} %bitcast.16, bf16[192,512]{1,0:T(8,128)(2,1)} %bitcast.15, s32[1,192]{1,0:T(1,128)} %bitcast.17), custom_call_target="tpu_custom_call" | custom-call | tf_op jit(solution)/shard_map/pallas_call | solution.py:354
  4.6 18.8 %all-to-all-start = ((bf16[64,8,1152]{2,1,0:T(8,128)(2,1)}), bf16[64,8,1152]{2,1,0:T(8,128)(2,1)}, u32[]{:S(2)}, u32[]{:S(2)}) async-start(bf16[64,8,1152]{2,1,0:T(8,128)(2,1)} %bitcast.5), calls=%async_computation | async-start | bytes 2359296 | tf_op jit(solution)/shard_map/all_to_all | solution.py:380
  23.4 1.9 %shard_map.69 = (bf16[3,1024,512]{2,1,0:T(8,128)(2,1)S(1)}, bf16[5,192,512]{2,1,0:T(8,128)(2,1)S(1)}) custom-call(bf16[3,1024,512]{2,1,0:T(8,128)(2,1)} %refs_0_.1, s32[1,192]{1,0:T(1,128)S(1)} %get-tuple-element.21.refs_1_), custom_call_target="tpu_custom_call" | custom-call | bytes 6000000 | tf_op jit(solution)/shard_map/pallas_call | solution.py:371
  25.3 0.0 copy-start
  25.4 1.0 copy-done
  26.3 57.9 %all-to-all-done = bf16[64,8,1152]{2,1,0:T(8,128)(2,1)} async-done(((bf16[64,8,1152]{2,1,0:T(8,128)(2,1)}), bf16[64,8,1152]{2,1,0:T(8,128)(2,1)}, u32[]{:S(2)}, u32[]{:S(2)}) %all-to-all-start) | async-done | bytes 1179680 | tf_op jit(solution)/shard_map/all_to_all | solution.py:380
  84.2 2.1 %collective-permute-start = (bf16[512,1152]{1,0:T(8,128)(2,1)}, bf16[512,1152]{1,0:T(8,128)(2,1)S(1)}, u32[]{:S(2)}, u32[]{:S(2)}) collective-permute-start(bf16[512,1152]{1,0:T(8,128)(2,1)} %bitcast.6.recv_ref), channel_id=1, source_target_pairs={{0,4},{4,0},{1,5},{5,1},{2,6},{6,2},{3,7},{7,3},{8,12},{12,8},{9,1... | collective-permute-start | bytes 3538952 | tf_op jit(solution)/shard_map/ppermute | solution.py:382
  86.3 2.7 %shard_map.70 = (bf16[576,512]{1,0:T(8,128)(2,1)S(1)}, bf16[576,512]{1,0:T(8,128)(2,1)S(1)}, f32[576,640]{1,0:T(8,128)S(1)}, f32[3,576,512]{2,1,0:T(8,128)S(1)}) custom-call(s32[1]{0:T(128)} %bitcast.refs_0_.head_ref, bf16[512,1152]{1,0:T(8,128)(2,1)} %bitcast.6.recv_ref, bf16[3,1024,512]{2,1,0:T(8,128)(2,1)S(1)} %get-tuple-element.25.weights_ref), custom_call_target="tpu_custom_call" | custom-call | bytes 6000000 | tf_op jit(solution)/shard_map/pallas_call | solution.py:303
  89.0 0.2 collective-permute-done.other_ref
  89.1 11.5 %shard_map.71 = (bf16[576,512]{1,0:T(8,128)(2,1)S(1)}, bf16[576,640]{1,0:T(8,128)(2,1)S(1)}, f32[576,128]{1,0:T(8,128)S(1)}) custom-call(s32[1]{0:T(128)} %bitcast.refs_0_.head_ref, bf16[512,1152]{1,0:T(8,128)(2,1)S(1)} %collective-permute-done.other_ref, bf16[576,512]{1,0:T(8,128)(2,1)S(1)} %get-tuple-element.26.own_ref, ...), custom_call_target="tpu_custom_call" | custom-call | tf_op jit(solution)/shard_map/pallas_call | solution.py:322
  100.6 2.5 %collective-permute-start.1 = (bf16[576,640]{1,0:T(8,128)(2,1)S(1)}, bf16[576,640]{1,0:T(8,128)(2,1)S(1)}, u32[]{:S(2)}, u32[]{:S(2)}) collective-permute-start(bf16[576,640]{1,0:T(8,128)(2,1)S(1)} %get-tuple-element.32), channel_id=1, source_target_pairs={{0,4},{4,0},{1,5},{5,1},{2,6},{6,2},{3,7},{7,3},{8,12},{12,8},{9,1... | collective-permute-start | bytes 2211848 | tf_op jit(solution)/shard_map/ppermute | solution.py:385
  103.1 1.6 collective-permute-done.1.got_ref
  104.7 0.0 copy-start.1
  104.7 1.0 shard_map.72
  105.7 44.6 %all_to_all.10 = bf16[64,8,640]{2,1,0:T(8,128)(2,1)S(1)} all-to-all(bf16[64,8,640]{2,1,0:T(8,128)(2,1)S(1)} %bitcast.12), channel_id=1, replica_groups=mesh['seq'=64,'head'=2,'dp'=4] {'seq'}, dimensions={0} | all-to-all | bytes 1310720 | tf_op jit(solution)/shard_map/all_to_all | solution.py:389
  150.3 0.0 copy-done.1
  150.3 1.3 shard_map.73
  151.6 11.3 %psum.7 = f32[512]{0:T(512)} all-reduce(f32[512]{0:T(512)S(1)} %bitcast.13), channel_id=1, replica_groups=mesh['seq'=64,'head'=2,'dp'=4] {'dp'}, use_global_device_ids=true, to_apply=%region_0.0 | all-reduce | flops 512 | bytes 4096 | tf_op jit(solution)/shard_map/psum | solution.py:396
Async XLA Ops:
  4.6 79.6 %all-to-all-start = ((bf16[64,8,1152]{2,1,0:T(8,128)(2,1)}), bf16[64,8,1152]{2,1,0:T(8,128)(2,1)}, u32[]{:S(2)}, u32[]{:S(2)}) async-start(bf16[64,8,1152]{2,1,0:T(8,128)(2,1)} %bitcast.5), calls=%async_computation | async-start | bytes 2359296 | tf_op jit(solution)/shard_map/all_to_all | solution.py:380
  25.3 1.0 copy-start
  84.2 4.9 %collective-permute-start = (bf16[512,1152]{1,0:T(8,128)(2,1)}, bf16[512,1152]{1,0:T(8,128)(2,1)S(1)}, u32[]{:S(2)}, u32[]{:S(2)}) collective-permute-start(bf16[512,1152]{1,0:T(8,128)(2,1)} %bitcast.6.recv_ref), channel_id=1, source_target_pairs={{0,4},{4,0},{1,5},{5,1},{2,6},{6,2},{3,7},{7,3},{8,12},{12,8},{9,1... | collective-permute-start | bytes 3538952 | tf_op jit(solution)/shard_map/ppermute | solution.py:382
  100.6 4.1 %collective-permute-start.1 = (bf16[576,640]{1,0:T(8,128)(2,1)S(1)}, bf16[576,640]{1,0:T(8,128)(2,1)S(1)}, u32[]{:S(2)}, u32[]{:S(2)}) collective-permute-start(bf16[576,640]{1,0:T(8,128)(2,1)S(1)} %get-tuple-element.32), channel_id=1, source_target_pairs={{0,4},{4,0},{1,5},{5,1},{2,6},{6,2},{3,7},{7,3},{8,12},{12,8},{9,1... | collective-permute-start | bytes 2211848 | tf_op jit(solution)/shard_map/ppermute | solution.py:385
  104.7 45.6 %copy-start.1 = (bf16[5,192,512]{2,1,0:T(8,128)(2,1)S(1)}, bf16[5,192,512]{2,1,0:T(8,128)(2,1)}, u32[]{:S(2)}) copy-start(bf16[5,192,512]{2,1,0:T(8,128)(2,1)} %copy-done) | copy-start | bytes 2949124

commit v5 on v3

--- a/solution.py
+++ b/solution.py
@@ -21,16 +21,17 @@
     return lax.broadcasted_iota(jnp.int32, shape, dim)
 
 
-def vmem_call(kernel, out_shape, scratch=(), limit=8, scalars=0, count=1, space=None):
+def vmem_call(kernel, out_shape, scratch=(), limit=8, scalars=0, count=1, space=pltpu.VMEM, cost=None):
     spec = pl.BlockSpec(memory_space=pltpu.VMEM)
-    source = spec if space is None else pl.BlockSpec(memory_space=space)
+    spaces = space if isinstance(space, tuple) else (space,) * count
     return pl.pallas_call(
         kernel,
         out_shape=out_shape,
-        in_specs=[pl.BlockSpec(memory_space=pltpu.SMEM)] * scalars + [source] * count,
+        in_specs=[pl.BlockSpec(memory_space=pltpu.SMEM)] * scalars + [pl.BlockSpec(memory_space=m) for m in spaces],
         out_specs=jax.tree.map(lambda _: spec, out_shape),
         scratch_shapes=scratch,
         compiler_params=pltpu.CompilerParams(vmem_limit_bytes=limit * 2**20),
+        cost_estimate=cost and pl.CostEstimate(flops=0, bytes_accessed=cost, transcendentals=0),
     )
 
 
@@ -102,44 +103,72 @@
     return high.astype(f32), middle.astype(f32), rest - middle.astype(f32)
 
 
-def attend_kernel(head_ref, recv_ref, other_ref, weights_ref, gain_ref, keep_ref, send_ref, own_ref, stats_ref,
-                  peer_ref, u_ref, q_ref, k_ref, v_ref, g_ref, dq_ref, bias_ref):
-    rows, extended = recv_ref.shape
+def own_kernel(slots, head_ref, recv_ref, weights_ref, labrow_ref, own_ref, u_ref, bias_ref, acc_ref, hot_ref):
+    rows = recv_ref.shape[0]
+    half = weights_ref.shape[2]
+    width = 2 * half
+    late = rows // 8
+    total = rows + late
+    pick_col, pick_row = iota((late, rows), 1), iota((late, rows), 0)
+    own_ref[late:, :] = recv_ref[:, :half]
+    u_ref[late:, :] = recv_ref[:, half:width]
+    for i in range(4):
+        span = slice(i * 128, (i + 1) * 128)
+        pick = (pick_col == pick_row * 8 + i).astype(bf16)
+        own_ref[:late, span] = dims(pick, recv_ref[:, width:], 1, 0).astype(bf16)
+        pick = (pick_col == pick_row * 8 + (i + 4)).astype(bf16)
+        u_ref[:late, span] = dims(pick, recv_ref[:, width:], 1, 0).astype(bf16)
+    up = u_ref[:, :128].astype(f32)
+    pads = up[:, :1] > 0.5 * PAD_MARK
+    u_ref[:, :128] = jnp.where(pads & (iota((total, 128), 1) == 0), 0.0, up).astype(bf16)
+    own_rows = pl.ds(pl.multiple_of(head_ref[0] * half, half), half)
+    own = own_ref[...]
+    for n in range(3):
+        acc_ref[n] = dims(own, weights_ref[n, own_rows, :], 1, 0)
+
+    def order(i):
+        return jnp.where(i < late, i * 9 + 8, ((i - late) >> 3) * 9 + ((i - late) & 7))
+
+    place = jnp.where(pads, 2 * total, order(iota((total, 1), 0)))
+    column = iota((1, rows), 1) + late
+    bias_ref[:, :rows] = jnp.where(place <= order(column), 0.0, MASKED)
+    column = iota((1, 2 * late), 1) & (late - 1)
+    bias_ref[:, rows:] = jnp.where(place <= order(column), 0.0, MASKED)
+    tokens = hot_ref.shape[1]
+    labrow = labrow_ref[...]
+    lab = column_of(labrow)
+    before = (lab == labrow) & (iota((tokens, tokens), 1) < iota((tokens, tokens), 0))
+    rank = jnp.sum(before.astype(f32), -1, keepdims=True).astype(jnp.int32)
+    key = jnp.where(rank < slots - 1, lab * 8 + rank, -1)
+    last = jnp.where(rank == slots - 1, lab, -1)
+    col = iota((tokens, rows), 1)
+    hot_last = jnp.where((col >> 3) == last, col & 7, -1)
+    hot_ref[4] = (col == key).astype(bf16)
+    for i in range(4):
+        hot_ref[i] = (hot_last == i).astype(bf16)
+
+
+def attend_kernel(head_ref, other_ref, own_ref, u_ref, bias_ref, acc_ref, weights_ref, gain_ref,
+                  keep_ref, send_ref, stats_ref, peer_ref, q_ref, k_ref, v_ref, g_ref, dq_ref):
+    rows = other_ref.shape[0]
     half = weights_ref.shape[2]
     width = 2 * half
     late = rows // 8
     total = rows + late
     head = head_ref[0]
     pick_col, pick_row = iota((late, rows), 1), iota((late, rows), 0)
-    own_ref[late:, :] = recv_ref[:, :half]
     peer_ref[late:, :] = other_ref[:, :half]
-    u_ref[late:, :] = recv_ref[:, half:width]
     for i in range(4):
-        span = slice(i * 128, (i + 1) * 128)
         pick = (pick_col == pick_row * 8 + i).astype(bf16)
-        own_ref[:late, span] = dims(pick, recv_ref[:, width:], 1, 0).astype(bf16)
-        peer_ref[:late, span] = dims(pick, other_ref[:, width:], 1, 0).astype(bf16)
-        pick = (pick_col == pick_row * 8 + (i + 4)).astype(bf16)
-        u_ref[:late, span] = dims(pick, recv_ref[:, width:], 1, 0).astype(bf16)
-    up = u_ref[:, :128].astype(f32)
-    pads = up[:, :1] > 0.5 * PAD_MARK
-    u_ref[:, :128] = jnp.where(pads & (iota((total, 128), 1) == 0), 0.0, up).astype(bf16)
+        peer_ref[:late, i * 128 : (i + 1) * 128] = dims(pick, other_ref[:, width:], 1, 0).astype(bf16)
     own_rows = pl.ds(pl.multiple_of(head * half, half), half)
     other_rows = pl.ds(pl.multiple_of((1 - head) * half, half), half)
     own, peer = own_ref[...], peer_ref[...]
     factor = HDIM**-0.5
     for n, ref in enumerate((q_ref, k_ref, v_ref)):
-        made = dims(own, weights_ref[n, own_rows, :], 1, 0) + dims(peer, weights_ref[n, other_rows, :], 1, 0)
+        made = acc_ref[n] + dims(peer, weights_ref[n, other_rows, :], 1, 0)
         ref[...] = (made * factor if n == 0 else made).astype(bf16)
 
-    def order(i):
-        return jnp.where(i < late, i * 9 + 8, ((i - late) >> 3) * 9 + ((i - late) & 7))
-
-    place = jnp.where(pads, 2 * total, order(iota((total, 1), 0)))
-    column = iota((1, rows), 1) + late
-    bias_ref[:, :rows] = jnp.where(place <= order(column), 0.0, MASKED)
-    column = iota((1, 2 * late), 1) & (late - 1)
-    bias_ref[:, rows:] = jnp.where(place <= order(column), 0.0, MASKED)
     left = iota((total, 2 * HDIM), 1) < HDIM
     block = rows // 2
     low = late + block
@@ -248,55 +277,58 @@
     out_ref[:, half:] = ext.astype(bf16)
 
 
-def finish_kernel(slots, scale, back_ref, labrow_ref, spread_ref, out_ref, gain_ref):
-    tokens, half = out_ref.shape
+def finish_kernel(scale, back_ref, hot_ref, spread_ref, out_ref, gain_ref):
+    half = out_ref.shape[1]
     rows = back_ref.shape[0]
-    labrow = labrow_ref[...]
-    lab = column_of(labrow)
-    before = (lab == labrow) & (iota((tokens, tokens), 1) < iota((tokens, tokens), 0))
-    rank = jnp.sum(before.astype(f32), -1, keepdims=True).astype(jnp.int32)
-    key = jnp.where(rank < slots - 1, lab * 8 + rank, -1)
-    last = jnp.where(rank == slots - 1, lab, -1)
-    col = iota((tokens, rows), 1)
-    hot = (col == key).astype(bf16)
-    hot_last = jnp.where((col >> 3) == last, col & 7, -1)
     spread = spread_ref[...]
     ext = back_ref[:, half:]
     piece = iota((rows, 128), 0) & 7
     for i in range(half // 128):
         span = slice(i * 128, (i + 1) * 128)
-        value = dims(hot, back_ref[:, span], 1, 0)
-        value = value + dims((hot_last == i).astype(bf16), ext, 1, 0)
+        value = dims(hot_ref[4], back_ref[:, span], 1, 0) + dims(hot_ref[i], ext, 1, 0)
         out_ref[:, span] = (value * spread).astype(bf16)
         gain_ref[:, span] = scale * jnp.sum(jnp.where(piece == i + 4, ext.astype(f32), 0.0), 0, keepdims=True)
 
 
-def attend_call(head, recv, peer, projection, gain):
+def own_call(slots, head, recv, projection, labrow):
     rows, half = recv.shape[0], projection.shape[2]
     total = rows + rows // 8
     shape = jax.ShapeDtypeStruct
     return vmem_call(
-        attend_kernel,
+        lambda *refs: own_kernel(slots, *refs),
         (
             shape((total, half), bf16),
-            shape((total, half + 128), bf16),
             shape((total, half), bf16),
-            shape((total, 128), f32),
+            shape((total, rows + 2 * (total - rows)), f32),
+            shape((3, total, half), f32),
+            shape((5, labrow.shape[1], rows), bf16),
         ),
+        limit=20,
+        cost=6 * 10**6,
+        scalars=1,
+        count=3,
+    )(head, recv, projection, labrow)
+
+
+def attend_call(head, peer, own, up, bias, acc, projection, gain):
+    rows, half = peer.shape[0], projection.shape[2]
+    total = rows + rows // 8
+    shape = jax.ShapeDtypeStruct
+    return vmem_call(
+        attend_kernel,
+        (shape((total, half), bf16), shape((total, half + 128), bf16), shape((total, 128), f32)),
         scratch=[
-            pltpu.VMEM((total, half), bf16),
             pltpu.VMEM((total, half), bf16),
             pltpu.VMEM((total, half), bf16),
             pltpu.VMEM((total, half), bf16),
             pltpu.VMEM((total, half), bf16),
             pltpu.VMEM((2, total, half), bf16),
             pltpu.VMEM((half, total), bf16),
-            pltpu.VMEM((total, rows + 2 * (total - rows)), f32),
         ],
         limit=26,
         scalars=1,
-        count=4,
-    )(head, recv, peer, projection, gain)
+        count=7,
+    )(head, peer, own, up, bias, acc, projection, gain)
 
 
 def on_device(hidden, norm_gain, projection, upstream, cluster):
@@ -332,7 +364,8 @@
     recv = lax.all_to_all(sent.reshape(sources, 8, width + 128), "seq", 0, 0, tiled=True)
     recv = recv.reshape(rows, width + 128)
     peer = lax.ppermute(recv, "head", swap)
-    keep, send, own, stats = attend_call(head, recv, peer, weights, gain)
+    own, up, bias, acc, hots = own_call(slots, head, recv, weights, labrow)
+    keep, send, stats = attend_call(head, peer, own, up, bias, acc, weights, gain)
     got = lax.ppermute(send, "head", swap)
     answer = vmem_call(combine_kernel, shape((rows, half + 128), bf16), scalars=1, count=5)(
         head, keep, got, own, stats, gain
@@ -340,10 +373,10 @@
     back = lax.all_to_all(answer.reshape(sources, 8, half + 128), "seq", 0, 0, tiled=True)
     back = back.reshape(rows, half + 128)
     result, gain_sum = vmem_call(
-        lambda *refs: finish_kernel(slots, scale, *refs),
+        lambda *refs: finish_kernel(scale, *refs),
         (shape((tokens, half), bf16), shape((1, half), f32)),
         count=3,
-    )(back, labrow, spread)
+    )(back, hots, spread)
     gain_gradient = lax.psum(gain_sum.reshape(half), "dp")
     return (result.reshape(1, tokens, half), gain_gradient)
 

time: 162 us -> 161 us (level)
  transfers between devices with their start and end apart: 2 -> 2, of which waited for: 2 -> 2; matrix products, arithmetic and copies ran while one was open for 0% -> 0% of each run, Pallas kernels for 0% -> 1%
where the time goes in v5:
time: 161 us
  blocking collectives  135 us (84%)
  Pallas kernels  17.8 us (11%)
  starting transfers between devices  4.35 us (3%)
  waiting for transfers between devices  2.92 us (2%)
    all_to_all x1, blocking collectives, on_device(): lax.all_to_all(sent.reshape(sources, 8, width + 128), 'seq', 0, 0, tiled=...  79.2 us
    all_to_all x1, blocking collectives, on_device(): lax.all_to_all(answer.reshape(sources, 8, half + 128), 'seq', 0, 0, tiled...  44.4 us
    pallas_call x1, Pallas kernels, attend_call(): vmem_call(attend_kernel, (shape((total, half), bf16), shape((total, half...  11.5 us
    psum x1, blocking collectives, on_device(): gain_gradient = lax.psum(gain_sum.reshape(half), 'dp')  11.3 us
  transfers between devices with their start and end apart: 2, of which 2 were waited for; matrix products, arithmetic and copies ran while one was open for 0% of the time, Pallas kernels for 1%

profile of v5, /device:TPU:2, one launch (start us, length us, event | category | flops | bytes accessed | tf_op | source)
XLA Modules:
  0.0 160.7 jit_solution(11685951057537732390)
XLA Ops:
  0.6 2.5 %shard_map.68 = (bf16[512,1152]{1,0:T(8,128)(2,1)S(1)}, f32[192,1]{1,0:T(8,128)S(1)}, f32[1,1024]{1,0:T(1,128)S(1)}, s32[1,192]{1,0:T(1,128)S(1)}, bf16[3,1024,512]{2,1,0:T(8,128)(2,1)S(1)}) custom-call(s32[1]{0:T(128)} %bitcast.refs_0_.head_ref, bf16[192,1024]{1,0:T(8,128)(2,1)} %bitcast.17, f32[1,1024]{1,0:T(1,128)} %bitcast.19, ...), custom_call_target="tpu_custom_call" | custom-call | tf_op jit(solution)/shard_map/pallas_call | solution.py:345
  3.1 79.2 %all_to_all.10 = bf16[64,8,1152]{2,1,0:T(8,128)(2,1)S(1)} all-to-all(bf16[64,8,1152]{2,1,0:T(8,128)(2,1)S(1)} %bitcast.15), channel_id=1, replica_groups=mesh['seq'=64,'head'=2,'dp'=4] {'seq'}, dimensions={0} | all-to-all | bytes 2359296 | tf_op jit(solution)/shard_map/all_to_all | solution.py:364
  82.4 2.1 %collective-permute-start = (bf16[512,1152]{1,0:T(8,128)(2,1)S(1)}, bf16[512,1152]{1,0:T(8,128)(2,1)S(1)}, u32[]{:S(2)}, u32[]{:S(2)}) collective-permute-start(bf16[512,1152]{1,0:T(8,128)(2,1)S(1)} %bitcast.11), channel_id=1, source_target_pairs={{0,4},{4,0},{1,5},{5,1},{2,6},{6,2},{3,7},{7,3},{8,12},{12,8},{9,1... | collective-permute-start | bytes 3538952 | tf_op jit(solution)/shard_map/ppermute | solution.py:366
  84.5 1.5 shard_map.69
  86.0 1.1 collective-permute-done.other_ref
  87.1 11.5 %shard_map.70 = (bf16[576,512]{1,0:T(8,128)(2,1)S(1)}, bf16[576,640]{1,0:T(8,128)(2,1)S(1)}, f32[576,128]{1,0:T(8,128)S(1)}) custom-call(s32[1]{0:T(128)} %bitcast.refs_0_.head_ref, bf16[512,1152]{1,0:T(8,128)(2,1)S(1)} %collective-permute-done.other_ref, bf16[576,512]{1,0:T(8,128)(2,1)S(1)} %get-tuple-element.20.own_ref, ...), custom_call_target="tpu_custom_call" | custom-call | tf_op jit(solution)/shard_map/pallas_call | solution.py:317
  98.6 2.3 %collective-permute-start.1 = (bf16[576,640]{1,0:T(8,128)(2,1)S(1)}, bf16[576,640]{1,0:T(8,128)(2,1)S(1)}, u32[]{:S(2)}, u32[]{:S(2)}) collective-permute-start(bf16[576,640]{1,0:T(8,128)(2,1)S(1)} %get-tuple-element.26), channel_id=1, source_target_pairs={{0,4},{4,0},{1,5},{5,1},{2,6},{6,2},{3,7},{7,3},{8,12},{12,8},{9,1... | collective-permute-start | bytes 2211848 | tf_op jit(solution)/shard_map/ppermute | solution.py:369
  100.8 1.8 %collective-permute-done.1.got_ref = bf16[576,640]{1,0:T(8,128)(2,1)S(1)} collective-permute-done((bf16[576,640]{1,0:T(8,128)(2,1)S(1)}, bf16[576,640]{1,0:T(8,128)(2,1)S(1)}, u32[]{:S(2)}, u32[]{:S(2)}) %collective-permute-start.1) | collective-permute-done | bytes 737312 | tf_op jit(solution)/shard_map/ppermute | solution.py:369
  102.7 1.0 shard_map.71
  103.7 44.4 %all_to_all.11 = bf16[64,8,640]{2,1,0:T(8,128)(2,1)S(1)} all-to-all(bf16[64,8,640]{2,1,0:T(8,128)(2,1)S(1)} %bitcast.14), channel_id=1, replica_groups=mesh['seq'=64,'head'=2,'dp'=4] {'seq'}, dimensions={0} | all-to-all | bytes 1310720 | tf_op jit(solution)/shard_map/all_to_all | solution.py:373
  148.0 1.3 shard_map.72
  149.4 11.3 %psum.7 = f32[512]{0:T(512)} all-reduce(f32[512]{0:T(512)S(1)} %bitcast.16), channel_id=1, replica_groups=mesh['seq'=64,'head'=2,'dp'=4] {'dp'}, use_global_device_ids=true, to_apply=%region_0.0 | all-reduce | flops 512 | bytes 4096 | tf_op jit(solution)/shard_map/psum | solution.py:380
Async XLA Ops:
  82.4 4.7 %collective-permute-start = (bf16[512,1152]{1,0:T(8,128)(2,1)S(1)}, bf16[512,1152]{1,0:T(8,128)(2,1)S(1)}, u32[]{:S(2)}, u32[]{:S(2)}) collective-permute-start(bf16[512,1152]{1,0:T(8,128)(2,1)S(1)} %bitcast.11), channel_id=1, source_target_pairs={{0,4},{4,0},{1,5},{5,1},{2,6},{6,2},{3,7},{7,3},{8,12},{12,8},{9,1... | collective-permute-start | bytes 3538952 | tf_op jit(solution)/shard_map/ppermute | solution.py:366
  98.6 4.1 %collective-permute-start.1 = (bf16[576,640]{1,0:T(8,128)(2,1)S(1)}, bf16[576,640]{1,0:T(8,128)(2,1)S(1)}, u32[]{:S(2)}, u32[]{:S(2)}) collective-permute-start(bf16[576,640]{1,0:T(8,128)(2,1)S(1)} %get-tuple-element.26), channel_id=1, source_target_pairs={{0,4},{4,0},{1,5},{5,1},{2,6},{6,2},{3,7},{7,3},{8,12},{12,8},{9,1... | collective-permute-start | bytes 2211848 | tf_op jit(solution)/shard_map/ppermute | solution.py:369

commit v6 on v5

--- a/solution.py
+++ b/solution.py
@@ -57,29 +57,29 @@
     ]
     for copy in copies:
         copy.start()
-    for copy in copies[:3]:
-        copy.wait()
+    copies[0].wait()
     tokens, width = hidden_ref.shape
     half = width // 2
+    rows = out_ref.shape[0]
+    labrow = labrow_ref[...]
+    lab = column_of(labrow)
+    before = (lab == labrow) & (iota((tokens, tokens), 0) < iota((tokens, tokens), 1))
+    rank = jnp.sum(before.astype(f32), 0, keepdims=True).astype(jnp.int32)
+    key = jnp.where(rank < slots - 1, labrow * 8 + rank, -1)
+    last = jnp.where(rank == slots - 1, labrow, -1)
+    row = iota((rows, tokens), 0)
+    hot = (row == key).astype(f32)
+    taken = jnp.sum(hot, -1, keepdims=True)
+    hot = hot.astype(bf16)
+    for copy in copies[1:4]:
+        copy.wait()
     x = hidden_ref[...].astype(f32)
     center = x - jnp.mean(x, -1, keepdims=True)
     spread = lax.rsqrt(jnp.mean(center * center, -1, keepdims=True) + EPSILON)
     spread_ref[...] = spread
     normed = (center * spread * gain_ref[...]).astype(bf16)
     own = jnp.where(head_ref[0] == 0, normed[:, :half], normed[:, half:])
-    copies[3].wait()
     up = up_ref[...]
-    labrow = labrow_ref[...]
-    lab = column_of(labrow)
-    before = (lab == labrow) & (iota((tokens, tokens), 0) < iota((tokens, tokens), 1))
-    rank = jnp.sum(before.astype(f32), 0, keepdims=True).astype(jnp.int32)
-    rows = out_ref.shape[0]
-    key = jnp.where(rank < slots - 1, labrow * 8 + rank, -1)
-    last = jnp.where(rank == slots - 1, labrow, -1)
-    row = iota((rows, tokens), 0)
-    hot = (row == key).astype(f32)
-    taken = jnp.sum(hot, -1, keepdims=True)
-    hot = hot.astype(bf16)
     out_ref[:, :half] = dims(hot, own, 1, 0).astype(bf16)
     right = dims(hot, up, 1, 0)
     first = iota((rows, half), 1) == 0

time: 161 us -> 161 us (level)
  no operation moved by 1% of the time
where the time goes in v6:
time: 161 us
  blocking collectives  135 us (84%)
  Pallas kernels  17.7 us (11%)
  starting transfers between devices  4.35 us (3%)
  waiting for transfers between devices  2.92 us (2%)
    all_to_all x1, blocking collectives, on_device(): lax.all_to_all(sent.reshape(sources, 8, width + 128), 'seq', 0, 0, tiled=...  79.2 us
    all_to_all x1, blocking collectives, on_device(): lax.all_to_all(answer.reshape(sources, 8, half + 128), 'seq', 0, 0, tiled...  44.4 us
    pallas_call x1, Pallas kernels, attend_call(): vmem_call(attend_kernel, (shape((total, half), bf16), shape((total, half...  11.5 us
    psum x1, blocking collectives, on_device(): gain_gradient = lax.psum(gain_sum.reshape(half), 'dp')  11.3 us
  transfers between devices with their start and end apart: 2, of which 2 were waited for; matrix products, arithmetic and copies ran while one was open for 0% of the time, Pallas kernels for 1%

profile of v6, /device:TPU:2, one launch (start us, length us, event | category | flops | bytes accessed | tf_op | source)
XLA Modules:
  0.0 160.5 jit_solution(5602817810079497072)
XLA Ops:
  0.6 2.4 %shard_map.68 = (bf16[512,1152]{1,0:T(8,128)(2,1)S(1)}, f32[192,1]{1,0:T(8,128)S(1)}, f32[1,1024]{1,0:T(1,128)S(1)}, s32[1,192]{1,0:T(1,128)S(1)}, bf16[3,1024,512]{2,1,0:T(8,128)(2,1)S(1)}) custom-call(s32[1]{0:T(128)} %bitcast.refs_0_.head_ref, bf16[192,1024]{1,0:T(8,128)(2,1)} %bitcast.17, f32[1,1024]{1,0:T(1,128)} %bitcast.19, ...), custom_call_target="tpu_custom_call" | custom-call | tf_op jit(solution)/shard_map/pallas_call | solution.py:345
  3.0 79.2 %all_to_all.10 = bf16[64,8,1152]{2,1,0:T(8,128)(2,1)S(1)} all-to-all(bf16[64,8,1152]{2,1,0:T(8,128)(2,1)S(1)} %bitcast.15), channel_id=1, replica_groups=mesh['seq'=64,'head'=2,'dp'=4] {'seq'}, dimensions={0} | all-to-all | bytes 2359296 | tf_op jit(solution)/shard_map/all_to_all | solution.py:364
  82.2 2.1 %collective-permute-start = (bf16[512,1152]{1,0:T(8,128)(2,1)S(1)}, bf16[512,1152]{1,0:T(8,128)(2,1)S(1)}, u32[]{:S(2)}, u32[]{:S(2)}) collective-permute-start(bf16[512,1152]{1,0:T(8,128)(2,1)S(1)} %bitcast.11), channel_id=1, source_target_pairs={{0,4},{4,0},{1,5},{5,1},{2,6},{6,2},{3,7},{7,3},{8,12},{12,8},{9,1... | collective-permute-start | bytes 3538952 | tf_op jit(solution)/shard_map/ppermute | solution.py:366
  84.3 1.5 shard_map.69
  85.9 1.1 collective-permute-done.other_ref
  87.0 11.5 %shard_map.70 = (bf16[576,512]{1,0:T(8,128)(2,1)S(1)}, bf16[576,640]{1,0:T(8,128)(2,1)S(1)}, f32[576,128]{1,0:T(8,128)S(1)}) custom-call(s32[1]{0:T(128)} %bitcast.refs_0_.head_ref, bf16[512,1152]{1,0:T(8,128)(2,1)S(1)} %collective-permute-done.other_ref, bf16[576,512]{1,0:T(8,128)(2,1)S(1)} %get-tuple-element.20.own_ref, ...), custom_call_target="tpu_custom_call" | custom-call | tf_op jit(solution)/shard_map/pallas_call | solution.py:317
  98.4 2.3 %collective-permute-start.1 = (bf16[576,640]{1,0:T(8,128)(2,1)S(1)}, bf16[576,640]{1,0:T(8,128)(2,1)S(1)}, u32[]{:S(2)}, u32[]{:S(2)}) collective-permute-start(bf16[576,640]{1,0:T(8,128)(2,1)S(1)} %get-tuple-element.26), channel_id=1, source_target_pairs={{0,4},{4,0},{1,5},{5,1},{2,6},{6,2},{3,7},{7,3},{8,12},{12,8},{9,1... | collective-permute-start | bytes 2211848 | tf_op jit(solution)/shard_map/ppermute | solution.py:369
  100.7 1.8 %collective-permute-done.1.got_ref = bf16[576,640]{1,0:T(8,128)(2,1)S(1)} collective-permute-done((bf16[576,640]{1,0:T(8,128)(2,1)S(1)}, bf16[576,640]{1,0:T(8,128)(2,1)S(1)}, u32[]{:S(2)}, u32[]{:S(2)}) %collective-permute-start.1) | collective-permute-done | bytes 737312 | tf_op jit(solution)/shard_map/ppermute | solution.py:369
  102.5 1.0 shard_map.71
  103.5 44.4 %all_to_all.11 = bf16[64,8,640]{2,1,0:T(8,128)(2,1)S(1)} all-to-all(bf16[64,8,640]{2,1,0:T(8,128)(2,1)S(1)} %bitcast.14), channel_id=1, replica_groups=mesh['seq'=64,'head'=2,'dp'=4] {'seq'}, dimensions={0} | all-to-all | bytes 1310720 | tf_op jit(solution)/shard_map/all_to_all | solution.py:373
  147.9 1.3 shard_map.72
  149.2 11.3 %psum.7 = f32[512]{0:T(512)} all-reduce(f32[512]{0:T(512)S(1)} %bitcast.16), channel_id=1, replica_groups=mesh['seq'=64,'head'=2,'dp'=4] {'dp'}, use_global_device_ids=true, to_apply=%region_0.0 | all-reduce | flops 512 | bytes 4096 | tf_op jit(solution)/shard_map/psum | solution.py:380
Async XLA Ops:
  82.2 4.7 %collective-permute-start = (bf16[512,1152]{1,0:T(8,128)(2,1)S(1)}, bf16[512,1152]{1,0:T(8,128)(2,1)S(1)}, u32[]{:S(2)}, u32[]{:S(2)}) collective-permute-start(bf16[512,1152]{1,0:T(8,128)(2,1)S(1)} %bitcast.11), channel_id=1, source_target_pairs={{0,4},{4,0},{1,5},{5,1},{2,6},{6,2},{3,7},{7,3},{8,12},{12,8},{9,1... | collective-permute-start | bytes 3538952 | tf_op jit(solution)/shard_map/ppermute | solution.py:366
  98.4 4.1 %collective-permute-start.1 = (bf16[576,640]{1,0:T(8,128)(2,1)S(1)}, bf16[576,640]{1,0:T(8,128)(2,1)S(1)}, u32[]{:S(2)}, u32[]{:S(2)}) collective-permute-start(bf16[576,640]{1,0:T(8,128)(2,1)S(1)} %get-tuple-element.26), channel_id=1, source_target_pairs={{0,4},{4,0},{1,5},{5,1},{2,6},{6,2},{3,7},{7,3},{8,12},{12,8},{9,1... | collective-permute-start | bytes 2211848 | tf_op jit(solution)/shard_map/ppermute | solution.py:369
